TPU v7x, 256 devices: a whole 4x4x8 slice. The times are simulated.
256 devices in a mesh: seg: 32 (over y, z), chan: 8 (over x, core).
Axes of the slice: x: 4, y: 4, z: 8, core: 2. Of those that a mesh axis runs over, the one named last changes fastest.
Arguments:
- ref_signals: bfloat16 [32, 524288], P('chan', 'seg'), may hold values from -6 to 6
- responses: bfloat16 [1024, 524288], P('chan', 'seg'), may hold values from -48 to 48
Outputs:
- transfer: float32 [512, 2, 32, 1024], P('seg', None, None, 'chan')
All inputs are finite; a program needn't handle non-finite values.
Results may differ from a plain program's by a relative error of at most 0.006.
Values may be sent and summed in bfloat16 or wider, within the bound.
No kernel may reach another device: no remote copies, remote signals or barrier semaphores. Data moves between devices by JAX's collectives and lax.ppermute only.
A program may use at most 128 MiB of HBM per device.

v0:
```python
import jax
import jax.numpy as jnp
from jax import lax
from jax.sharding import PartitionSpec as P

L = 2048
FB = 512


def dft_table(length, line_count):
    sample_idx = jnp.arange(length, dtype=jnp.int32)[:, None]
    line_idx = jnp.arange(line_count, dtype=jnp.int32)[None, :]
    phases = (sample_idx * line_idx % length).astype(jnp.float32) * (2.0 * jnp.pi / length)
    window = 0.5 - 0.5 * jnp.cos(
        jnp.arange(length, dtype=jnp.int32).astype(jnp.float32) * (2.0 * jnp.pi / length)
    )
    cos_part = window[:, None] * jnp.cos(phases)
    sin_part = -window[:, None] * jnp.sin(phases)
    return (
        jnp.stack([cos_part, sin_part], axis=2).reshape(length, 2 * line_count).astype(jnp.bfloat16)
    )


def transform(signal, kernel):
    blocks = signal.reshape(signal.shape[0], signal.shape[1] // L, L)
    return jnp.einsum("rsn,nj->jsr", blocks, kernel, preferred_element_type=jnp.float32).astype(
        jnp.bfloat16
    )


def contract(left_op, right_op):
    return jnp.einsum("fsa,fsb->fab", left_op, right_op, preferred_element_type=jnp.float32)


def cross_terms(ref_spectra, resp_spectra):
    ref_split = ref_spectra.reshape(
        ref_spectra.shape[0] // 2, 2, ref_spectra.shape[1], ref_spectra.shape[2]
    )
    resp_split = resp_spectra.reshape(
        resp_spectra.shape[0] // 2, 2, resp_spectra.shape[1], resp_spectra.shape[2]
    )
    ref_real, ref_imag = (ref_split[:, 0], ref_split[:, 1])
    resp_real, resp_imag = (resp_split[:, 0], resp_split[:, 1])
    auto_sums = jnp.stack(
        [
            contract(ref_real, ref_real) + contract(ref_imag, ref_imag),
            contract(ref_real, ref_imag) - contract(ref_imag, ref_real),
        ],
        1,
    )
    crossed = jnp.stack(
        [
            contract(ref_real, resp_real) + contract(ref_imag, resp_imag),
            contract(ref_real, resp_imag) - contract(ref_imag, resp_real),
        ],
        1,
    )
    return (auto_sums, crossed)


def solve_lines(auto_sums, cross_sums):
    real_part = auto_sums[:, 0]
    imag_part = auto_sums[:, 1]
    real_form = jnp.concatenate(
        [jnp.concatenate([real_part, -imag_part], 2), jnp.concatenate([imag_part, real_part], 2)], 1
    )
    right_side = jnp.concatenate([cross_sums[:, 0], cross_sums[:, 1]], 1)
    factor = jnp.linalg.cholesky(real_form)
    solved = jax.scipy.linalg.cho_solve((factor, True), right_side)
    return solved.reshape(solved.shape[0], 2, solved.shape[1] // 2, solved.shape[2])


def local(ref_signals, responses):
    kernel = dft_table(L, FB)
    resp_spectra = transform(responses, kernel)
    ref_spectra = transform(lax.all_gather(ref_signals, "chan", axis=0, tiled=True), kernel)
    auto_sums, crossed = cross_terms(ref_spectra, resp_spectra)
    auto_sums, crossed = (
        lax.psum_scatter(auto_sums, "seg", scatter_dimension=0, tiled=True),
        lax.psum_scatter(crossed, "seg", scatter_dimension=0, tiled=True),
    )
    return solve_lines(auto_sums, crossed)


def solution(mesh):
    placed = (P("chan", "seg"), P("chan", "seg"))
    return jax.shard_map(
        local, mesh=mesh, in_specs=placed, out_specs=P("seg", None, None, "chan"), check_vma=False
    )
```

profile of v0, /device:TPU:2, one launch (start us, length us, event | category | flops | bytes accessed | tf_op | source)
XLA Modules:
  0.0 580.8 jit_solution(8960330054642083290)
XLA Ops:
  7.4 17.7 %multiply_convert_fusion = (bf16[2048,512,1]{1,0,2:T(8,128)(2,1)S(1)}, bf16[2048,512,1]{1,0,2:T(8,128)(2,1)S(1)}) fusion(f32[2048]{0:T(1024)S(1)} %fusion.33, f32[2048]{0:T(1024)S(1)} %multiply_subtract_fusion), kind=kLoop, calls=%fused_computation.19 | loop fusion | flops 18874368 | bytes 4210688 | tf_op jit(solution)/shard_map/convert.1
  25.1 2.3 pad_maximum_fusion.2
  27.4 11.4 %copy.51 = bf16[2048,512,2]{0,2,1:T(2,128)(2,1)} copy(bf16[2048,512,2]{1,0,2:T(8,128)(2,1)} %pad_maximum_fusion.2) | data formatting | bytes 8388608 | tf_op jit(solution)/shard_map/stack | solution.py:20
  38.8 7.2 %convert_element_type.56 = bf16[2048,1024]{0,1:T(8,128)(2,1)} reshape(bf16[2048,512,2]{0,2,1:T(2,128)(2,1)} %copy.51) | data formatting | bytes 8388608 | tf_op jit(solution)/shard_map/convert_element_type | solution.py:20
  46.0 1.8 reshape.169
  47.8 4.0 fusion.17
  51.8 1.6 copy.54
  58.9 6.3 %pad_maximum_fusion = f32[512,2,32,32]{3,2,0,1:T(8,128)} fusion(f32[512,1,32,32]{3,2,0,1:T(8,128)S(1)} %subtract_bitcast_fusion.1, f32[512,1,32,32]{3,2,0,1:T(8,128)S(1)} %add_bitcast_fusion.1), kind=kLoop, calls=%fused_computation.1 | loop fusion | flops 1048576 | bytes 8388608 | tf_op jit(solution)/shard_map/stack | solution.py:44
  65.2 17.7 %copy.66 = f32[512,2,32,32]{2,3,1,0:T(8,128)} copy(f32[512,2,32,32]{3,2,0,1:T(8,128)} %pad_maximum_fusion) | data formatting | bytes 8388608
  82.9 13.4 %reshape.180 = f32[512,2048]{1,0:T(8,128)} reshape(f32[512,2,32,32]{3,2,1,0:T(8,128)} %bitcast.115) | data formatting | bytes 8388608
  96.6 7.2 %reshape.178 = bf16[2048,1024,1]{0,1,2:T(8,128)(2,1)} reshape(bf16[2048,512,2]{0,2,1:T(2,128)(2,1)} %copy.51) | data formatting | bytes 8388608 | tf_op jit(solution)/shard_map/convert_element_type | solution.py:20
  103.8 7.6 %fusion.11 = bf16[1024,128,8]{1,0,2:T(8,128)(2,1)S(1)} fusion(bf16[2048,1024,1]{0,1,2:T(8,128)(2,1)} %reshape.178, bf16[16,8,8,2048]{3,2,1,0:T(8,128)(2,1)} %bitcast.124), kind=kOutput, calls=%fused_computation.24 | convolution fusion | flops 4296015872 | bytes 10485760 | tf_op jit(solution)/shard_map/rsn,nj->jsr/dot_general | solution.py:26
  111.4 3.0 fusion.36
  114.4 1.6 fusion.21
  116.0 1.6 fusion.22
  117.6 4.5 subtract_bitcast_fusion
  122.1 5.3 add_bitcast_fusion
  128.4 4.9 pad_maximum_fusion.1
  133.3 1.6 copy.68
  134.9 18.0 %copy.97 = f32[64,8,64,128]{3,1,2,0:T(8,128)} copy(f32[64,8,64,128]{3,2,1,0:T(8,128)S(1)} %bitcast.117) | data formatting | bytes 33554432
  153.0 168.0 %reduce-scatter.8.cloned.1.call-done = f32[16,2048]{1,0:T(8,128)} async-done(((f32[512,2048]{1,0:T(8,128)}), f32[16,2048]{1,0:T(8,128)}) %reduce-scatter.8.cloned.1.call-update) | async-done | bytes 131088
  322.7 93.8 %custom-call.11 = f32[16,64,64]{2,1,0:T(8,128)S(1)} custom-call(f32[16,64,64]{2,1,0:T(8,128)S(1)} %fusion.32), custom_call_target="Cholesky" | custom-call | tf_op jit(solution)/shard_map/jit(cholesky)/cholesky | solution.py:68
  416.8 78.6 %custom-call.12 = f32[16,1,64,64]{2,3,1,0:T(8,128)S(1)} custom-call(f32[16,1,64,64]{3,2,1,0:T(8,128)S(1)} %select_bitcast_fusion), custom_call_target="InvertDiagBlocksLowerTriangular" | custom-call | tf_op jit(solution)/shard_map/jit(_cho_solve)/vmap()/triangular_solve | solution.py:69
  495.5 75.2 %reduce-scatter.10.cloned.1.call-done = f32[16,8192]{1,0:T(8,128)} async-done(((f32[512,8192]{1,0:T(8,128)}), f32[16,8192]{1,0:T(8,128)}) %reduce-scatter.10.cloned.1.call-update) | async-done | bytes 524304
  (30 shorter events, 13.2 us)
Async XLA Ops:
  6.5 39.4 %all-gather.3.cloned.1.call-start = ((), (), s32[]{:S(2)}) async-start(), calls=%async_computation.2 | async-start | bytes 1179648 | tf_op jit(solution)/shard_map/all_gather | solution.py:76
  7.3 313.7 %reduce-scatter.8.cloned.1.call-start = ((), (), s32[]{:S(2)}) async-start(), calls=%async_computation.3 | async-start | bytes 4325376
  96.3 474.3 %reduce-scatter.10.cloned.1.call-start = ((), (), s32[]{:S(2)}) async-start(), calls=%async_computation.4 | async-start | bytes 17301504
  122.1 6.3 %copy-start = (f32[512,1,32,128]{3,2,0,1:T(8,128)S(1)}, f32[512,1,32,128]{3,2,0,1:T(8,128)}, u32[]{:S(2)}) copy-start(f32[512,1,32,128]{3,2,0,1:T(8,128)} %subtract_bitcast_fusion) | copy-start | bytes 25165828
Sparse Core Ops, SparseCore 0:
  9.2 27.1 all-gather.2
  96.5 224.4 reduce-scatter.7
  325.6 244.9 reduce-scatter.9
where the time goes:
time: 582 us; the launch traced here: 581 us
  waiting for transfers between devices  244 us (42%)
  other arithmetic  204 us (35%)
  local copies, waits for them, and re-layouts  86.4 us (15%)
  matrix products  32.4 us (6%)
  between operations  13.3 us (2%)
    unnamed x5, waiting for transfers between devices  244 us
    another operation x4, other arithmetic, solve_lines(): factor = jnp.linalg.cholesky(real_form)  94 us
    another operation x3, other arithmetic, solve_lines(): solved = jax.scipy.linalg.cho_solve((factor, True), right_side)  78.8 us
    unnamed x8, local copies, waits for them, and re-layouts  54 us
    dot_general x8, matrix products, contract(): jnp.einsum('fsa,fsb->fab', left_op, right_op, preferred_element_type=jnp....  18.4 us
    another operation x1, other arithmetic  17.7 us
    convert_element_type x2, local copies, waits for them, and re-layouts, dft_table(): jnp.stack([cos_part, sin_part], axis=2).reshape(length, 2 * line_count)  14.4 us
  transfers between devices with their start and end apart: 3, of which 2 were waited for; matrix products, arithmetic and copies ran while one was open for 46% of the time, Pallas kernels for 0%

commit v1 on v0

v1 whole, which is shorter than its diff:
```python
import jax
import jax.numpy as jnp
import numpy as np
from jax import lax
from jax.experimental import pallas as pl
from jax.experimental.pallas import tpu as pltpu
from jax.sharding import PartitionSpec as P

L = 2048
FB = 512
NSEG = 32
NCHAN = 8
S = 8
LN = FB // NSEG
R = 32
RL = R // NCHAN
CL = 128
ROWS = 2 * S
DEPTH = NSEG * ROWS


def dft_table():
    n = np.arange(L, dtype=np.int64)[None, :]
    k = np.arange(FB, dtype=np.int64)[:, None]
    phase = (n * k % L) * (2.0 * np.pi / L)
    window = 0.5 - 0.5 * np.cos(n * (2.0 * np.pi / L))
    table = np.stack([window * np.cos(phase), -window * np.sin(phase)], axis=1)
    return jnp.asarray(table.reshape(2 * FB, L), dtype=jnp.bfloat16)


def transform_kernel(table_ref, resp_ref, ref_ref, out_ref, mixed):
    step = pl.program_id(0)
    block = resp_ref[...]
    pair = jnp.concatenate([block[:, :L], block[:, L:]], axis=0)
    for q in range(4):
        rows = slice(q * 256, (q + 1) * 256)
        lines = lax.dot_general(
            table_ref[rows, :], pair, (((1,), (1,)), ((), ())), preferred_element_type=jnp.float32
        )
        for i in range(2):
            mixed[pl.ds(q * 256 * S + 2 * step + i, 256, stride=S), :] = lines[:, i * CL : (i + 1) * CL]

    @pl.when(step == S // 2 - 1)
    def _():
        for d in range(NSEG):
            rows = LN * ROWS
            out_ref[d, 0:rows, :] = mixed[d * rows : (d + 1) * rows, :].astype(jnp.bfloat16)
        spec = lax.dot_general(
            ref_ref[...], table_ref[...], (((1,), (1,)), ((), ())), preferred_element_type=jnp.float32
        )
        for d in range(NSEG):
            parts = [spec[r * S : (r + 1) * S, d * 2 * LN : (d + 1) * 2 * LN] for r in range(RL)]
            tile = jnp.concatenate(parts, axis=1)
            out_ref[d, LN * ROWS :, :] = jnp.concatenate([tile, jnp.zeros_like(tile)], axis=0).astype(jnp.bfloat16)


def transform(table, responses, refs):
    return pl.pallas_call(
        transform_kernel,
        grid=(S // 2,),
        in_specs=[
            pl.BlockSpec((2 * FB, L), lambda i: (0, 0)),
            pl.BlockSpec((CL, 2 * L), lambda i: (0, i)),
            pl.BlockSpec((RL * S, L), lambda i: (0, 0)),
        ],
        out_specs=pl.BlockSpec((NSEG, (LN + 1) * ROWS, CL), lambda i: (0, 0, 0)),
        out_shape=jax.ShapeDtypeStruct((NSEG, (LN + 1) * ROWS, CL), jnp.bfloat16),
        scratch_shapes=[pltpu.VMEM((2 * FB * S, CL), jnp.float32)],
        compiler_params=pltpu.CompilerParams(vmem_limit_bytes=48 * 1024 * 1024),
    )(table, responses, refs)


def spots(shape, target):
    row = lax.broadcasted_iota(jnp.int32, shape, 0)
    column = lax.broadcasted_iota(jnp.int32, shape, 1)
    return jnp.where(column == target(row), 1.0, 0.0).astype(jnp.bfloat16)


def exact(left, right, dims):
    return lax.dot_general(left, right, (dims, ((), ())), preferred_element_type=jnp.float32).astype(jnp.bfloat16)


def solve_kernel(resp_ref, ref_ref, out_ref, auto, cross):
    wide = jnp.concatenate([ref_ref[c] for c in range(NCHAN)], axis=1)
    halves = []
    for part in range(2):
        pick = spots(
            (LN * R, NCHAN * 128),
            lambda i: (i // RL) % NCHAN * 128 + i % RL * (2 * LN) + i // R * 2 + part,
        )
        halves.append(exact(pick, wide, ((1,), (1,))))
    real, imag = halves
    put = [spots((NSEG * S, DEPTH), lambda i: i // S * ROWS + part * S + i % S) for part in range(2)]
    inner = ((1,), (0,))
    upper = exact(real, put[0], inner) + exact(imag, put[1], inner)
    lower = exact(real, put[1], inner) - exact(imag, put[0], inner)
    for k in range(LN):
        rows = slice(k * R, (k + 1) * R)
        both = jnp.concatenate([upper[rows], lower[rows]], axis=0)
        lines = resp_ref[:, k * ROWS : (k + 1) * ROWS, :].reshape(DEPTH, CL)
        cross[k] = jnp.dot(both, lines, preferred_element_type=jnp.float32)
        own = lax.dot_general(both, upper[rows], (((1,), (1,)), ((), ())), preferred_element_type=jnp.float32)
        auto[k] = jnp.concatenate([own[:R], own[R:]], axis=1)
    row = lax.broadcasted_iota(jnp.int32, (1, R, 1), 1)
    for k in range(R):
        a = auto[...]
        pivot = auto[:, k : k + 1, :]
        inverse = 1.0 / pivot[:, :, k : k + 1]
        turned = jnp.concatenate([-pivot[:, :, R:], pivot[:, :, :R]], axis=2)
        gain_r = jnp.where(row == k, 0.0, a[:, :, k : k + 1] * inverse)
        gain_i = jnp.where(row == k, 0.0, a[:, :, R + k : R + k + 1] * inverse)
        auto[...] = a - gain_r * pivot - gain_i * turned
        right_r = cross[:, k : k + 1, :]
        right_i = cross[:, R + k : R + k + 1, :]
        cross[:, :R, :] = cross[:, :R, :] - gain_r * right_r + gain_i * right_i
        cross[:, R:, :] = cross[:, R:, :] - gain_r * right_i - gain_i * right_r
    column = lax.broadcasted_iota(jnp.int32, (1, R, 2 * R), 2)
    diagonal = jnp.sum(jnp.where(column == lax.broadcasted_iota(jnp.int32, (1, R, 2 * R), 1), auto[...], 0.0), axis=2, keepdims=True)
    scale = 1.0 / diagonal
    out_ref[:, 0] = cross[:, :R, :] * scale
    out_ref[:, 1] = cross[:, R:, :] * scale


def solve(lines, refs):
    return pl.pallas_call(
        solve_kernel,
        out_shape=jax.ShapeDtypeStruct((LN, 2, R, CL), jnp.float32),
        in_specs=[pl.BlockSpec(memory_space=pltpu.VMEM)] * 2,
        out_specs=pl.BlockSpec(memory_space=pltpu.VMEM),
        scratch_shapes=[pltpu.VMEM((LN, R, 2 * R), jnp.float32), pltpu.VMEM((LN, 2 * R, CL), jnp.float32)],
        compiler_params=pltpu.CompilerParams(vmem_limit_bytes=48 * 1024 * 1024),
    )(lines, refs)


def local(ref_signals, responses):
    sent = transform(dft_table(), responses, ref_signals.reshape(RL * S, L))
    lines = lax.all_to_all(sent, "seg", 0, 0, tiled=True)
    refs = lax.all_gather(lines[:, LN * ROWS : LN * ROWS + S, :].reshape(NSEG * S, 128), "chan")
    return solve(lines, refs)


def solution(mesh):
    placed = (P("chan", "seg"), P("chan", "seg"))
    return jax.shard_map(
        local, mesh=mesh, in_specs=placed, out_specs=P("seg", None, None, "chan"), check_vma=False
    )
```

time: 582 us -> 103 us (0.18)
  waiting for transfers between devices: 244 us -> 0 us
  other arithmetic: 204 us -> 0 us
  local copies, waits for them, and re-layouts: 86.4 us -> 0.98 us
  blocking collectives: 0 us -> 79.9 us
  matrix products: 32.4 us -> 0 us
  Pallas kernels: 0 us -> 20.3 us
  between operations: 13.3 us -> 0.01 us
    unnamed x5 -> x0, waiting for transfers between devices: 244 us -> none
    another operation x11 -> x0, other arithmetic: 204 us -> none  [the longest x4 94 us: solve_lines(): factor = jnp.linalg.cholesky(real_form)]
    all_to_all x0 -> x1, blocking collectives: none -> 66.7 us  [local(): lines = lax.all_to_all(sent, 'seg', 0, 0, tiled=True)]
    unnamed x8 -> x0, local copies, waits for them, and re-layouts: 54 us -> none
    dot_general x10 -> x0, matrix products: 30 us -> none  [the longest x8 18.4 us: contract(): jnp.einsum('fsa,fsb->fab', left_op, right_op, preferred_element_type=jnp....]
    pallas_call x0 -> x2, Pallas kernels: none -> 20.3 us  [the longest x1 10.7 us: solve(): pl.pallas_call(solve_kernel, out_shape=jax.ShapeDtypeStruct((LN, 2, R, CL...]
    convert_element_type x3 -> x0, local copies, waits for them, and re-layouts: 16.1 us -> none  [the longest x2 14.4 us: dft_table(): jnp.stack([cos_part, sin_part], axis=2).reshape(length, 2 * line_count)]
    all_gather x0 -> x1, blocking collectives: none -> 13.1 us  [local(): lax.all_gather(lines[:, LN * ROWS:LN * ROWS + S, :].reshape(NSEG * S, 128...]
  transfers between devices with their start and end apart: 3 -> 0, of which waited for: 2 -> 0; matrix products, arithmetic and copies ran while one was open for 46% -> 0% of each run, Pallas kernels for 0% -> 0%
where the time goes in v1:
time: 103 us; the launch traced here: 101 us
  blocking collectives  79.9 us (78%)
  Pallas kernels  20.3 us (20%)
    all_to_all x1, blocking collectives, local(): lines = lax.all_to_all(sent, 'seg', 0, 0, tiled=True)  66.7 us
    all_gather x1, blocking collectives, local(): lax.all_gather(lines[:, LN * ROWS:LN * ROWS + S, :].reshape(NSEG * S, 128...  13.1 us
    pallas_call x1, Pallas kernels, solve(): pl.pallas_call(solve_kernel, out_shape=jax.ShapeDtypeStruct((LN, 2, R, CL...  10.7 us
    pallas_call x1, Pallas kernels, transform(): pl.pallas_call(transform_kernel, grid=(S // 2,), in_specs=[pl.BlockSpec((...  9.57 us

profile of v1, /device:TPU:2, one launch (start us, length us, event | category | flops | bytes accessed | tf_op | source)
XLA Modules:
  0.0 101.2 jit_solution(10851257549686965621)
XLA Ops:
  0.0 1.0 reshape.3.ref_ref
  1.0 9.6 %shard_map.37 = bf16[32,272,128]{2,1,0:T(8,128)(2,1)S(1)} custom-call(bf16[1024,2048]{1,0:T(8,128)(2,1)} %constant.2.clone.table_ref, bf16[128,16384]{1,0:T(8,128)(2,1)} %resp_ref.1, bf16[32,2048]{1,0:T(8,128)(2,1)S(1)} %reshape.3.ref_ref), custom_call_target="tpu_custom_call" | custom-call | tf_op jit(solution)/shard_map/pallas_call | solution.py:58
  10.6 66.7 %all_to_all.5.resp_ref = bf16[32,272,128]{2,1,0:T(8,128)(2,1)S(1)} all-to-all(bf16[32,272,128]{2,1,0:T(8,128)(2,1)S(1)} %shard_map.37), channel_id=1, replica_groups=mesh['seg'=32,'chan'=8] {'seg'}, dimensions={0} | all-to-all | bytes 4456448 | tf_op jit(solution)/shard_map/all_to_all | solution.py:137
  77.3 13.1 %all_gather.3.ref_ref = bf16[8,256,128]{2,1,0:T(8,128)(2,1)S(1)} all-gather(bf16[1,256,128]{2,1,0:T(8,128)(2,1)S(1)} %slice_bitcast_fusion), channel_id=1, replica_groups=mesh['seg'=32,'chan'=8] {'chan'}, dimensions={0}, use_global_device_ids=true | all-gather | bytes 589824 | tf_op jit(solution)/shard_map/all_gather | solution.py:138
  90.4 10.7 %shard_map.38 = f32[16,2,32,128]{3,2,1,0:T(8,128)} custom-call(bf16[32,272,128]{2,1,0:T(8,128)(2,1)S(1)} %all_to_all.5.resp_ref, bf16[8,256,128]{2,1,0:T(8,128)(2,1)S(1)} %all_gather.3.ref_ref), custom_call_target="tpu_custom_call" | custom-call | tf_op jit(solution)/shard_map/pallas_call | solution.py:125
  (1 shorter events, 0.0 us)

commit v2 on v1

v2 whole, which is shorter than its diff:
```python
import jax
import jax.numpy as jnp
import numpy as np
from jax import lax
from jax.experimental import pallas as pl
from jax.experimental.pallas import tpu as pltpu
from jax.sharding import PartitionSpec as P

L = 2048
FB = 512
NSEG = 32
NCHAN = 8
S = 8
LN = FB // NSEG
R = 32
RL = R // NCHAN
CL = 128
ROWS = 2 * S
DEPTH = NSEG * ROWS
VMEM_LIMIT = 60 * 1024 * 1024


def dft_table():
    n = np.arange(L, dtype=np.int64)[None, :]
    k = np.arange(FB, dtype=np.int64)[:, None]
    phase = (n * k % L) * (2.0 * np.pi / L)
    window = 0.5 - 0.5 * np.cos(n * (2.0 * np.pi / L))
    table = np.stack([window * np.cos(phase), -window * np.sin(phase)], axis=1)
    return jnp.asarray(table.reshape(2 * FB, L), dtype=jnp.bfloat16)


def whole():
    return pl.BlockSpec(memory_space=pltpu.VMEM)


def cost(flops, nbytes):
    return pl.CostEstimate(flops=flops, bytes_accessed=nbytes, transcendentals=0)


def params():
    return pltpu.CompilerParams(vmem_limit_bytes=VMEM_LIMIT)


def away():
    return pl.BlockSpec(memory_space=pl.ANY)


def fetch(pairs, sems):
    copies = [pltpu.make_async_copy(src, dst, sems.at[i]) for i, (src, dst) in enumerate(pairs)]
    for copy in copies:
        copy.start()
    return copies


def transform_kernel(table_hbm, resp_hbm, out_hbm, table, resp, mixed, out, sems, out_sems):
    cuts, pairs = 4, S // 2
    rows, some = 2 * FB // cuts, NSEG // cuts
    wanted = [(resp_hbm.at[:, pl.ds(0, 2 * L)], resp.at[0])]
    wanted += [(table_hbm.at[pl.ds(q * rows, rows)], table.at[pl.ds(q * rows, rows)]) for q in range(cuts)]
    wanted += [(resp_hbm.at[:, pl.ds(2 * p * L, 2 * L)], resp.at[p]) for p in range(1, pairs)]
    copies = fetch(wanted, sems)
    sent = []
    for p in range(pairs):
        copies[p + cuts if p else 0].wait()
        pair = jnp.concatenate([resp[p, :, :L], resp[p, :, L:]], axis=0)
        for q in range(cuts):
            if p == 0:
                copies[1 + q].wait()
            lines = lax.dot_general(
                table[q * rows : (q + 1) * rows, :], pair, (((1,), (1,)), ((), ())), preferred_element_type=jnp.float32
            )
            for i in range(2):
                mixed[pl.ds(q * rows * S + 2 * p + i, rows, stride=S), :] = lines[:, i * CL : (i + 1) * CL]
            if p == pairs - 1:
                for d in range(q * some, (q + 1) * some):
                    out[d] = mixed[d * LN * ROWS : (d + 1) * LN * ROWS, :].astype(jnp.bfloat16)
                part = pl.ds(q * some, some)
                sent.append(pltpu.make_async_copy(out.at[part], out_hbm.at[part], out_sems.at[q]))
                sent[-1].start()
    for copy in sent:
        copy.wait()


def transform(table, responses):
    out = (NSEG, LN * ROWS, CL)
    return pl.pallas_call(
        transform_kernel,
        in_specs=[away(), away()],
        out_specs=away(),
        out_shape=jax.ShapeDtypeStruct(out, jnp.bfloat16),
        scratch_shapes=[
            pltpu.VMEM((2 * FB, L), jnp.bfloat16),
            pltpu.VMEM((S // 2, CL, 2 * L), jnp.bfloat16),
            pltpu.VMEM((2 * FB * S, CL), jnp.float32),
            pltpu.VMEM(out, jnp.bfloat16),
            pltpu.SemaphoreType.DMA((8,)),
            pltpu.SemaphoreType.DMA((4,)),
        ],
        compiler_params=params(),
        cost_estimate=cost(2 * 2 * FB * L * CL * S, 12_000_000),
    )(table, responses)


def ref_kernel(table_hbm, ref_ref, out_ref, table, sems):
    cuts = 4
    rows, some = 2 * FB // cuts, NSEG // cuts
    copies = fetch([(table_hbm.at[pl.ds(q * rows, rows)], table.at[pl.ds(q * rows, rows)]) for q in range(cuts)], sems)
    x = ref_ref[...].astype(jnp.float32)
    x = jnp.concatenate([x[r : r + 1, s * L : (s + 1) * L] for r in range(RL) for s in range(S)], axis=0)
    x = x.astype(jnp.bfloat16)
    w = LN * 2
    for q in range(cuts):
        copies[q].wait()
        spec = lax.dot_general(
            x, table[q * rows : (q + 1) * rows, :], (((1,), (1,)), ((), ())), preferred_element_type=jnp.float32
        )
        for d in range(some):
            tile = jnp.concatenate([spec[r * S : (r + 1) * S, d * w : (d + 1) * w] for r in range(RL)], axis=1)
            out_ref[q * some + d] = jnp.concatenate([tile, jnp.zeros_like(tile)], axis=0).astype(jnp.bfloat16)


def ref_transform(table, refs):
    return pl.pallas_call(
        ref_kernel,
        in_specs=[away(), whole()],
        out_specs=whole(),
        out_shape=jax.ShapeDtypeStruct((NSEG, ROWS, 128), jnp.bfloat16),
        scratch_shapes=[pltpu.VMEM((2 * FB, L), jnp.bfloat16), pltpu.SemaphoreType.DMA((4,))],
        compiler_params=params(),
        cost_estimate=cost(2 * 2 * FB * L * RL * S, 5_000_000),
    )(table, refs)


def spots(shape, target):
    row = lax.broadcasted_iota(jnp.int32, shape, 0)
    column = lax.broadcasted_iota(jnp.int32, shape, 1)
    return jnp.where(column == target(row), 1.0, 0.0).astype(jnp.bfloat16)


def exact(left, right, dims):
    return lax.dot_general(left, right, (dims, ((), ())), preferred_element_type=jnp.float32).astype(jnp.bfloat16)


def three(a):
    parts = []
    for _ in range(3):
        parts.append(a.astype(jnp.bfloat16))
        a = a - parts[-1].astype(jnp.float32)
    return parts


def invert_kernel(ref_ref, out_ref, left, state):
    wide = jnp.concatenate([ref_ref[c] for c in range(NCHAN)], axis=1)
    halves = []
    for part in range(2):
        pick = spots(
            (LN * R, NCHAN * 128),
            lambda i: (i // RL) % NCHAN * 128 + i % RL * (2 * LN) + i // R * 2 + part,
        )
        halves.append(exact(pick, wide, ((1,), (1,))))
    real, imag = halves
    put = [spots((NSEG * S, DEPTH), lambda i: i // S * ROWS + part * S + i % S) for part in range(2)]
    inner = ((1,), (0,))
    upper = exact(real, put[0], inner) + exact(imag, put[1], inner)
    lower = exact(real, put[1], inner) - exact(imag, put[0], inner)
    row = lax.broadcasted_iota(jnp.int32, (R, R), 0)
    column = lax.broadcasted_iota(jnp.int32, (R, R), 1)
    unit = jnp.where(row == column, 1.0, 0.0)
    for k in range(LN):
        rows = slice(k * R, (k + 1) * R)
        both = jnp.concatenate([upper[rows], lower[rows]], axis=0)
        left[k] = both
        own = lax.dot_general(both, upper[rows], (((1,), (1,)), ((), ())), preferred_element_type=jnp.float32)
        state[k] = jnp.concatenate([own[:R], own[R:], unit, jnp.zeros_like(unit)], axis=1)
    row = lax.broadcasted_iota(jnp.int32, (1, R, 1), 1)
    for k in range(R):
        a = state[...]
        pivot = state[:, k : k + 1, :]
        scale = 1.0 / pivot[:, :, k : k + 1]
        turned = jnp.concatenate(
            [-pivot[:, :, R : 2 * R], pivot[:, :, :R], -pivot[:, :, 3 * R :], pivot[:, :, 2 * R : 3 * R]], axis=2
        )
        gain_r = jnp.where(row == k, 0.0, a[:, :, k : k + 1] * scale)
        gain_i = jnp.where(row == k, 0.0, a[:, :, R + k : R + k + 1] * scale)
        state[...] = a - gain_r * pivot - gain_i * turned
    a = state[...]
    row = lax.broadcasted_iota(jnp.int32, (1, R, 4 * R), 1)
    column = lax.broadcasted_iota(jnp.int32, (1, R, 4 * R), 2)
    a = a * (1.0 / jnp.sum(jnp.where(column == row, a, 0.0), axis=2, keepdims=True))
    inv_r, inv_i = a[:, :, 2 * R : 3 * R], a[:, :, 3 * R :]
    for k in range(LN):
        inverse = jnp.concatenate(
            [
                jnp.concatenate([inv_r[k], -inv_i[k]], axis=1),
                jnp.concatenate([inv_i[k], inv_r[k]], axis=1),
            ],
            axis=0,
        )
        terms = jnp.dot(jnp.concatenate(three(inverse), axis=0), left[k], preferred_element_type=jnp.float32)
        terms = terms[: 2 * R] + (terms[2 * R : 4 * R] + terms[4 * R :])
        out_ref[k] = jnp.concatenate(three(terms), axis=0)


def invert(refs):
    return pl.pallas_call(
        invert_kernel,
        out_shape=jax.ShapeDtypeStruct((LN, 6 * R, DEPTH), jnp.bfloat16),
        in_specs=[whole()],
        out_specs=whole(),
        scratch_shapes=[pltpu.VMEM((LN, 2 * R, DEPTH), jnp.bfloat16), pltpu.VMEM((LN, R, 4 * R), jnp.float32)],
        compiler_params=params(),
        cost_estimate=cost(6_000_000_000, 2_000_000),
    )(refs)


def apply_kernel(resp_hbm, left_hbm, out_hbm, resp, left, out, sems, out_sems):
    cuts = 4
    some = LN // cuts
    wanted = []
    for q in range(cuts):
        part, rows = pl.ds(q * some, some), pl.ds(q * some * ROWS, some * ROWS)
        wanted += [(left_hbm.at[part], left.at[part]), (resp_hbm.at[:, rows], resp.at[:, rows])]
    copies = fetch(wanted, sems)
    sent = []
    for q in range(cuts):
        copies[2 * q].wait()
        copies[2 * q + 1].wait()
        for k in range(q * some, (q + 1) * some):
            lines = resp[:, k * ROWS : (k + 1) * ROWS, :].reshape(DEPTH, CL)
            terms = jnp.dot(left[k], lines, preferred_element_type=jnp.float32)
            found = terms[: 2 * R] + (terms[2 * R : 4 * R] + terms[4 * R :])
            out[k, 0] = found[:R]
            out[k, 1] = found[R:]
        part = pl.ds(q * some, some)
        sent.append(pltpu.make_async_copy(out.at[part], out_hbm.at[part], out_sems.at[q]))
        sent[-1].start()
    for copy in sent:
        copy.wait()


def apply(lines, left):
    out = (LN, 2, R, CL)
    return pl.pallas_call(
        apply_kernel,
        out_shape=jax.ShapeDtypeStruct(out, jnp.float32),
        in_specs=[away(), away()],
        out_specs=away(),
        scratch_shapes=[
            pltpu.VMEM((NSEG, LN * ROWS, CL), jnp.bfloat16),
            pltpu.VMEM((LN, 6 * R, DEPTH), jnp.bfloat16),
            pltpu.VMEM(out, jnp.float32),
            pltpu.SemaphoreType.DMA((8,)),
            pltpu.SemaphoreType.DMA((4,)),
        ],
        compiler_params=params(),
        cost_estimate=cost(2_000_000_000, 4_000_000),
    )(lines, left)


def local(ref_signals, responses):
    table = dft_table()
    tiles = ref_transform(table, ref_signals)
    tiles, responses = lax.optimization_barrier((tiles, responses))
    tiles = lax.all_to_all(tiles, "seg", 0, 0, tiled=True)
    lines = lax.all_to_all(transform(table, responses), "seg", 0, 0, tiled=True)
    refs = lax.all_gather(tiles[:, :S, :].reshape(NSEG * S, 128), "chan")
    return apply(lines, invert(refs))


def solution(mesh):
    placed = (P("chan", "seg"), P("chan", "seg"))
    return jax.shard_map(
        local, mesh=mesh, in_specs=placed, out_specs=P("seg", None, None, "chan"), check_vma=False
    )
```

time: 103 us -> 91.9 us (0.89); the launches traced: 101 us -> 91.6 us
  blocking collectives: 79.9 us -> 14.4 us
  waiting for transfers between devices: 0 us -> 21.5 us
  starting transfers between devices: 0 us -> 20.8 us
  Pallas kernels: 20.3 us -> 33.4 us
    all_to_all x1 -> x0, blocking collectives: 66.7 us -> none  [local(): lines = lax.all_to_all(sent, 'seg', 0, 0, tiled=True)]
    all_to_all x0 -> x2, waiting for transfers between devices: none -> 21.5 us  [the longest x1 21 us: local(): lines = lax.all_to_all(transform(table, responses), 'seg', 0, 0, tiled=True)]
    all_to_all x0 -> x2, starting transfers between devices: none -> 20.8 us  [the longest x1 11.5 us: local(): tiles = lax.all_to_all(tiles, 'seg', 0, 0, tiled=True)]
    pallas_call x2 -> x4, Pallas kernels: 20.3 us -> 33.4 us  [the longest x1 14.2 us: invert(): pl.pallas_call(invert_kernel, out_shape=jax.ShapeDtypeStruct((LN, 6 * R,...]
    unnamed x0 -> x2, local copies, waits for them, and re-layouts: none -> 1.35 us
    all_gather x1, blocking collectives: 13.1 us -> 14.4 us  [local(): refs = lax.all_gather(tiles[:, :S, :].reshape(NSEG * S, 128), 'chan')]
  transfers between devices with their start and end apart: 0 -> 2, of which waited for: 0 -> 2; matrix products, arithmetic and copies ran while one was open for 0% -> 0% of each run, Pallas kernels for 0% -> 26%
where the time goes in v2:
time: 91.9 us; the launch traced here: 91.6 us
  Pallas kernels  33.4 us (36%)
  waiting for transfers between devices  21.5 us (23%)
  starting transfers between devices  20.8 us (23%)
  blocking collectives  14.4 us (16%)
  local copies, waits for them, and re-layouts  1.35 us (1%)
    all_to_all x1, waiting for transfers between devices, local(): lines = lax.all_to_all(transform(table, responses), 'seg', 0, 0, tiled=True)  21 us
    all_gather x1, blocking collectives, local(): refs = lax.all_gather(tiles[:, :S, :].reshape(NSEG * S, 128), 'chan')  14.4 us
    pallas_call x1, Pallas kernels, invert(): pl.pallas_call(invert_kernel, out_shape=jax.ShapeDtypeStruct((LN, 6 * R,...  14.2 us
    all_to_all x1, starting transfers between devices, local(): tiles = lax.all_to_all(tiles, 'seg', 0, 0, tiled=True)  11.5 us
    pallas_call x1, Pallas kernels, transform(): pl.pallas_call(transform_kernel, in_specs=[away(), away()], out_specs=awa...  9.76 us
    all_to_all x1, starting transfers between devices, local(): lines = lax.all_to_all(transform(table, responses), 'seg', 0, 0, tiled=True)  9.3 us
    pallas_call x1, Pallas kernels, ref_transform(): pl.pallas_call(ref_kernel, in_specs=[away(), whole()], out_specs=whole(),...  5.77 us
    pallas_call x1, Pallas kernels, apply(): pl.pallas_call(apply_kernel, out_shape=jax.ShapeDtypeStruct(out, jnp.floa...  3.58 us
  transfers between devices with their start and end apart: 2, of which 2 were waited for; matrix products, arithmetic and copies ran while one was open for 0% of the time, Pallas kernels for 26%

profile of v2, /device:TPU:2, one launch (start us, length us, event | category | flops | bytes accessed | tf_op | source)
XLA Modules:
  0.0 91.6 jit_solution(733922716013095020)
XLA Ops:
  0.0 5.8 %shard_map.37 = bf16[32,16,128]{2,1,0:T(8,128)(2,1)} custom-call(bf16[1024,2048]{1,0:T(8,128)(2,1)} %constant.2.clone.table_hbm, bf16[4,16384]{1,0:T(4,128)(2,1)} %ref_ref.1), custom_call_target="tpu_custom_call" | custom-call | flops 134217728 | bytes 5000000 | tf_op jit(solution)/shard_map/pallas_call | solution.py:123
  5.8 11.5 %all-to-all-start.1 = ((bf16[32,16,128]{2,1,0:T(8,128)(2,1)}), bf16[32,16,128]{2,1,0:T(8,128)(2,1)S(1)}, u32[]{:S(2)}, u32[]{:S(2)}) async-start(bf16[32,16,128]{2,1,0:T(8,128)(2,1)} %shard_map.37), calls=%async_computation.1 | async-start | bytes 262144 | tf_op jit(solution)/shard_map/all_to_all | solution.py:264
  17.3 9.8 %shard_map.38 = bf16[32,256,128]{2,1,0:T(8,128)(2,1)} custom-call(bf16[1024,2048]{1,0:T(8,128)(2,1)} %constant.2.clone.table_hbm, bf16[128,16384]{1,0:T(8,128)(2,1)} %resp_hbm), custom_call_target="tpu_custom_call" | custom-call | flops 4294967296 | bytes 12000000 | tf_op jit(solution)/shard_map/pallas_call | solution.py:86
  27.1 0.5 all-to-all-done.1
  27.6 9.3 %all-to-all-start = ((bf16[32,256,128]{2,1,0:T(8,128)(2,1)}), bf16[32,256,128]{2,1,0:T(8,128)(2,1)S(1)}, u32[]{:S(2)}, u32[]{:S(2)}) async-start(bf16[32,256,128]{2,1,0:T(8,128)(2,1)} %shard_map.38), calls=%async_computation | async-start | bytes 4194304 | tf_op jit(solution)/shard_map/all_to_all | solution.py:265
  36.9 14.4 %all_gather.3.ref_ref = bf16[8,256,128]{2,1,0:T(8,128)(2,1)} all-gather(bf16[1,256,128]{2,1,0:T(8,128)(2,1)S(1)} %slice_bitcast_fusion), channel_id=1, replica_groups=mesh['seg'=32,'chan'=8] {'chan'}, dimensions={0}, use_global_device_ids=true | all-gather | bytes 589824 | tf_op jit(solution)/shard_map/all_gather | solution.py:266
  51.3 14.2 %shard_map.39.left_hbm = bf16[16,192,512]{2,1,0:T(8,128)(2,1)} custom-call(bf16[8,256,128]{2,1,0:T(8,128)(2,1)} %all_gather.3.ref_ref), custom_call_target="tpu_custom_call" | custom-call | flops 6000000000 | bytes 2000000 | tf_op jit(solution)/shard_map/pallas_call | solution.py:205
  65.6 21.0 %all-to-all-done.resp_hbm = bf16[32,256,128]{2,1,0:T(8,128)(2,1)S(1)} async-done(((bf16[32,256,128]{2,1,0:T(8,128)(2,1)}), bf16[32,256,128]{2,1,0:T(8,128)(2,1)S(1)}, u32[]{:S(2)}, u32[]{:S(2)}) %all-to-all-start) | async-done | bytes 2097184 | tf_op jit(solution)/shard_map/all_to_all | solution.py:265
  86.5 0.0 copy-start
  86.5 1.3 %copy-done = bf16[32,256,128]{2,1,0:T(8,128)(2,1)} copy-done((bf16[32,256,128]{2,1,0:T(8,128)(2,1)}, bf16[32,256,128]{2,1,0:T(8,128)(2,1)S(1)}, u32[]{:S(2)}) %copy-start) | copy-done | bytes 2097176
  87.9 3.6 %shard_map.40 = f32[16,2,32,128]{3,2,1,0:T(8,128)} custom-call(bf16[32,256,128]{2,1,0:T(8,128)(2,1)} %copy-done, bf16[16,192,512]{2,1,0:T(8,128)(2,1)} %shard_map.39.left_hbm), custom_call_target="tpu_custom_call" | custom-call | flops 2000000000 | bytes 4000000 | tf_op jit(solution)/shard_map/pallas_call | solution.py:243
  (1 shorter events, 0.0 us)
Async XLA Ops:
  5.8 21.8 %all-to-all-start.1 = ((bf16[32,16,128]{2,1,0:T(8,128)(2,1)}), bf16[32,16,128]{2,1,0:T(8,128)(2,1)S(1)}, u32[]{:S(2)}, u32[]{:S(2)}) async-start(bf16[32,16,128]{2,1,0:T(8,128)(2,1)} %shard_map.37), calls=%async_computation.1 | async-start | bytes 262144 | tf_op jit(solution)/shard_map/all_to_all | solution.py:264
  27.6 59.0 %all-to-all-start = ((bf16[32,256,128]{2,1,0:T(8,128)(2,1)}), bf16[32,256,128]{2,1,0:T(8,128)(2,1)S(1)}, u32[]{:S(2)}, u32[]{:S(2)}) async-start(bf16[32,256,128]{2,1,0:T(8,128)(2,1)} %shard_map.38), calls=%async_computation | async-start | bytes 4194304 | tf_op jit(solution)/shard_map/all_to_all | solution.py:265
  86.5 1.3 %copy-start = (bf16[32,256,128]{2,1,0:T(8,128)(2,1)}, bf16[32,256,128]{2,1,0:T(8,128)(2,1)S(1)}, u32[]{:S(2)}) copy-start(bf16[32,256,128]{2,1,0:T(8,128)(2,1)S(1)} %all-to-all-done.resp_hbm) | copy-start | bytes 6291460

commit v3 on v2

--- a/solution.py
+++ b/solution.py
@@ -17,7 +17,7 @@
 CL = 128
 ROWS = 2 * S
 DEPTH = NSEG * ROWS
-VMEM_LIMIT = 60 * 1024 * 1024
+NY, NZ = 4, 8
 
 
 def dft_table():
@@ -37,8 +37,8 @@
     return pl.CostEstimate(flops=flops, bytes_accessed=nbytes, transcendentals=0)
 
 
-def params():
-    return pltpu.CompilerParams(vmem_limit_bytes=VMEM_LIMIT)
+def params(mib=60):
+    return pltpu.CompilerParams(vmem_limit_bytes=mib * 1024 * 1024)
 
 
 def away():
@@ -101,22 +101,33 @@
     )(table, responses)
 
 
-def ref_kernel(table_hbm, ref_ref, out_ref, table, sems):
-    cuts = 4
+def ref_kernel(table_hbm, ref_ref, out_ref, table, refs, sems):
+    cuts = 2
     rows, some = 2 * FB // cuts, NSEG // cuts
-    copies = fetch([(table_hbm.at[pl.ds(q * rows, rows)], table.at[pl.ds(q * rows, rows)]) for q in range(cuts)], sems)
+
+    def piece(q):
+        part = pl.ds(q * rows, rows)
+        return pltpu.make_async_copy(table_hbm.at[part], table.at[part], sems.at[q])
+
+    for q in range(cuts):
+        piece(q).start()
     x = ref_ref[...].astype(jnp.float32)
     x = jnp.concatenate([x[r : r + 1, s * L : (s + 1) * L] for r in range(RL) for s in range(S)], axis=0)
-    x = x.astype(jnp.bfloat16)
+    refs[...] = x.astype(jnp.bfloat16)
     w = LN * 2
-    for q in range(cuts):
-        copies[q].wait()
+
+    def body(q, carry):
+        piece(q).wait()
         spec = lax.dot_general(
-            x, table[q * rows : (q + 1) * rows, :], (((1,), (1,)), ((), ())), preferred_element_type=jnp.float32
+            refs[...], table[pl.ds(q * rows, rows), :], (((1,), (1,)), ((), ())), preferred_element_type=jnp.float32
         )
         for d in range(some):
             tile = jnp.concatenate([spec[r * S : (r + 1) * S, d * w : (d + 1) * w] for r in range(RL)], axis=1)
-            out_ref[q * some + d] = jnp.concatenate([tile, jnp.zeros_like(tile)], axis=0).astype(jnp.bfloat16)
+            tile = jnp.concatenate([tile, jnp.zeros_like(tile)], axis=0)
+            out_ref[d % NZ, q * (some // NZ) + d // NZ] = tile.astype(jnp.bfloat16)
+        return carry
+
+    lax.fori_loop(0, cuts, body, 0)
 
 
 def ref_transform(table, refs):
@@ -124,11 +135,26 @@
         ref_kernel,
         in_specs=[away(), whole()],
         out_specs=whole(),
-        out_shape=jax.ShapeDtypeStruct((NSEG, ROWS, 128), jnp.bfloat16),
-        scratch_shapes=[pltpu.VMEM((2 * FB, L), jnp.bfloat16), pltpu.SemaphoreType.DMA((4,))],
+        out_shape=jax.ShapeDtypeStruct((NZ, NY, ROWS, 128), jnp.bfloat16),
+        scratch_shapes=[
+            pltpu.VMEM((2 * FB, L), jnp.bfloat16),
+            pltpu.VMEM((RL * S, L), jnp.bfloat16),
+            pltpu.SemaphoreType.DMA((2,)),
+        ],
         compiler_params=params(),
         cost_estimate=cost(2 * 2 * FB * L * RL * S, 5_000_000),
     )(table, refs)
+
+
+def gather_refs(tiles):
+    y = lax.axis_index("seg") // NZ
+    got = []
+    for dy in range(NY):
+        slab = lax.dynamic_index_in_dim(tiles, (y + dy) % NY, 1, keepdims=False)
+        if dy:
+            slab = lax.ppermute(slab, "seg", [(i, (i + dy * NZ) % NSEG) for i in range(NSEG)])
+        got.append(slab[:, :S])
+    return lax.all_gather(jnp.stack(got).reshape(NSEG * S, 128), "chan")
 
 
 def spots(shape, target):
@@ -149,7 +175,8 @@
     return parts
 
 
-def invert_kernel(ref_ref, out_ref, left, state):
+def invert_kernel(y_ref, ref_ref, out_ref, left, state):
+    y = y_ref[0]
     wide = jnp.concatenate([ref_ref[c] for c in range(NCHAN)], axis=1)
     halves = []
     for part in range(2):
@@ -159,7 +186,7 @@
         )
         halves.append(exact(pick, wide, ((1,), (1,))))
     real, imag = halves
-    put = [spots((NSEG * S, DEPTH), lambda i: i // S * ROWS + part * S + i % S) for part in range(2)]
+    put = [spots((NSEG * S, DEPTH), lambda i: (((y - i // (NZ * S) + NY) % NY * NZ + i // S % NZ) * ROWS + part * S + i % S)) for part in range(2)]
     inner = ((1,), (0,))
     upper = exact(real, put[0], inner) + exact(imag, put[1], inner)
     lower = exact(real, put[1], inner) - exact(imag, put[0], inner)
@@ -201,58 +228,34 @@
         out_ref[k] = jnp.concatenate(three(terms), axis=0)
 
 
-def invert(refs):
+def invert(y, refs):
     return pl.pallas_call(
         invert_kernel,
         out_shape=jax.ShapeDtypeStruct((LN, 6 * R, DEPTH), jnp.bfloat16),
-        in_specs=[whole()],
+        in_specs=[pl.BlockSpec(memory_space=pltpu.SMEM), whole()],
         out_specs=whole(),
         scratch_shapes=[pltpu.VMEM((LN, 2 * R, DEPTH), jnp.bfloat16), pltpu.VMEM((LN, R, 4 * R), jnp.float32)],
         compiler_params=params(),
         cost_estimate=cost(6_000_000_000, 2_000_000),
-    )(refs)
-
-
-def apply_kernel(resp_hbm, left_hbm, out_hbm, resp, left, out, sems, out_sems):
-    cuts = 4
-    some = LN // cuts
-    wanted = []
-    for q in range(cuts):
-        part, rows = pl.ds(q * some, some), pl.ds(q * some * ROWS, some * ROWS)
-        wanted += [(left_hbm.at[part], left.at[part]), (resp_hbm.at[:, rows], resp.at[:, rows])]
-    copies = fetch(wanted, sems)
-    sent = []
-    for q in range(cuts):
-        copies[2 * q].wait()
-        copies[2 * q + 1].wait()
-        for k in range(q * some, (q + 1) * some):
-            lines = resp[:, k * ROWS : (k + 1) * ROWS, :].reshape(DEPTH, CL)
-            terms = jnp.dot(left[k], lines, preferred_element_type=jnp.float32)
-            found = terms[: 2 * R] + (terms[2 * R : 4 * R] + terms[4 * R :])
-            out[k, 0] = found[:R]
-            out[k, 1] = found[R:]
-        part = pl.ds(q * some, some)
-        sent.append(pltpu.make_async_copy(out.at[part], out_hbm.at[part], out_sems.at[q]))
-        sent[-1].start()
-    for copy in sent:
-        copy.wait()
+    )(y, refs)
+
+
+def apply_kernel(resp_ref, left_ref, out_ref):
+    for k in range(LN):
+        lines = resp_ref[:, k * ROWS : (k + 1) * ROWS, :].reshape(DEPTH, CL)
+        terms = jnp.dot(left_ref[k], lines, preferred_element_type=jnp.float32)
+        found = terms[: 2 * R] + (terms[2 * R : 4 * R] + terms[4 * R :])
+        out_ref[k, 0] = found[:R]
+        out_ref[k, 1] = found[R:]
 
 
 def apply(lines, left):
-    out = (LN, 2, R, CL)
     return pl.pallas_call(
         apply_kernel,
-        out_shape=jax.ShapeDtypeStruct(out, jnp.float32),
-        in_specs=[away(), away()],
-        out_specs=away(),
-        scratch_shapes=[
-            pltpu.VMEM((NSEG, LN * ROWS, CL), jnp.bfloat16),
-            pltpu.VMEM((LN, 6 * R, DEPTH), jnp.bfloat16),
-            pltpu.VMEM(out, jnp.float32),
-            pltpu.SemaphoreType.DMA((8,)),
-            pltpu.SemaphoreType.DMA((4,)),
-        ],
-        compiler_params=params(),
+        out_shape=jax.ShapeDtypeStruct((LN, 2, R, CL), jnp.float32),
+        in_specs=[whole(), whole()],
+        out_specs=whole(),
+        compiler_params=params(12),
         cost_estimate=cost(2_000_000_000, 4_000_000),
     )(lines, left)
 
@@ -261,10 +264,13 @@
     table = dft_table()
     tiles = ref_transform(table, ref_signals)
     tiles, responses = lax.optimization_barrier((tiles, responses))
-    tiles = lax.all_to_all(tiles, "seg", 0, 0, tiled=True)
-    lines = lax.all_to_all(transform(table, responses), "seg", 0, 0, tiled=True)
-    refs = lax.all_gather(tiles[:, :S, :].reshape(NSEG * S, 128), "chan")
-    return apply(lines, invert(refs))
+    along_z = [[y * NZ + z for z in range(NZ)] for y in range(NY)]
+    tiles = lax.all_to_all(tiles, "seg", 0, 0, axis_index_groups=along_z, tiled=True)
+    sent = transform(table, responses)
+    sent, tiles = lax.optimization_barrier((sent, tiles))
+    lines = lax.all_to_all(sent, "seg", 0, 0, tiled=True)
+    y = (lax.axis_index("seg") // NZ).astype(jnp.int32).reshape(1)
+    return apply(lines, invert(y, gather_refs(tiles)))
 
 
 def solution(mesh):

time: 91.9 us -> 87 us (0.947)
  waiting for transfers between devices: 21.5 us -> 15.9 us
  Pallas kernels: 33.4 us -> 30.7 us
  starting transfers between devices: 20.8 us -> 23.5 us
    all_to_all x2, waiting for transfers between devices: 21.5 us -> 11.6 us  [the longest x1 11.6 us: local(): lines = lax.all_to_all(sent, 'seg', 0, 0, tiled=True)]
    ppermute x0 -> x3, starting transfers between devices: none -> 4.8 us  [gather_refs(): lax.ppermute(slab, 'seg', [(i, (i + dy * NZ) % NSEG) for i in range(NSEG)])]
    ppermute x0 -> x3, waiting for transfers between devices: none -> 4.3 us  [gather_refs(): lax.ppermute(slab, 'seg', [(i, (i + dy * NZ) % NSEG) for i in range(NSEG)])]
    all_to_all x2, starting transfers between devices: 20.8 us -> 18.7 us  [the longest x1 10.2 us: local(): lines = lax.all_to_all(sent, 'seg', 0, 0, tiled=True)]
    pallas_call x1, Pallas kernels: 3.58 us -> 1.76 us  [apply(): pl.pallas_call(apply_kernel, out_shape=jax.ShapeDtypeStruct((LN, 2, R, CL...]
    pallas_call x1, Pallas kernels: 5.77 us -> 4.81 us  [ref_transform(): pl.pallas_call(ref_kernel, in_specs=[away(), whole()], out_specs=whole(),...]
  transfers between devices with their start and end apart: 2 -> 5, of which waited for: 2 -> 4; matrix products, arithmetic and copies ran while one was open for 0% -> 0% of each run, Pallas kernels for 26% -> 28%
where the time goes in v3:
time: 87 us; the launch traced here: 86.6 us
  Pallas kernels  30.7 us (35%)
  starting transfers between devices  23.5 us (27%)
  waiting for transfers between devices  15.9 us (18%)
  blocking collectives  14.4 us (17%)
  local copies, waits for them, and re-layouts  1.93 us (2%)
    all_gather x1, blocking collectives, gather_refs(): return lax.all_gather(jnp.stack(got).reshape(NSEG * S, 128), 'chan')  14.4 us
    pallas_call x1, Pallas kernels, invert(): pl.pallas_call(invert_kernel, out_shape=jax.ShapeDtypeStruct((LN, 6 * R,...  14.4 us
    all_to_all x1, waiting for transfers between devices, local(): lines = lax.all_to_all(sent, 'seg', 0, 0, tiled=True)  11.6 us
    all_to_all x1, starting transfers between devices, local(): lines = lax.all_to_all(sent, 'seg', 0, 0, tiled=True)  10.2 us
    pallas_call x1, Pallas kernels, transform(): pl.pallas_call(transform_kernel, in_specs=[away(), away()], out_specs=awa...  9.74 us
    all_to_all x1, starting transfers between devices, local(): lax.all_to_all(tiles, 'seg', 0, 0, axis_index_groups=along_z, tiled=True)  8.48 us
    pallas_call x1, Pallas kernels, ref_transform(): pl.pallas_call(ref_kernel, in_specs=[away(), whole()], out_specs=whole(),...  4.81 us
    ppermute x3, starting transfers between devices, gather_refs(): lax.ppermute(slab, 'seg', [(i, (i + dy * NZ) % NSEG) for i in range(NSEG)])  4.8 us
  transfers between devices with their start and end apart: 5, of which 4 were waited for; matrix products, arithmetic and copies ran while one was open for 0% of the time, Pallas kernels for 28%

profile of v3, /device:TPU:2, one launch (start us, length us, event | category | flops | bytes accessed | tf_op | source)
XLA Modules:
  0.0 86.6 jit_solution(4858805215573017589)
XLA Ops:
  0.0 4.8 %shard_map.37 = bf16[8,4,16,128]{3,2,1,0:T(8,128)(2,1)} custom-call(bf16[1024,2048]{1,0:T(8,128)(2,1)} %constant.63.clone.table_hbm, bf16[4,16384]{1,0:T(4,128)(2,1)} %ref_ref.1), custom_call_target="tpu_custom_call" | custom-call | flops 134217728 | bytes 5000000 | tf_op jit(solution)/shard_map/pallas_call | solution.py:134
  4.8 8.5 %all-to-all-start = ((bf16[8,4,16,128]{3,2,1,0:T(8,128)(2,1)}), bf16[8,4,16,128]{3,2,1,0:T(8,128)(2,1)S(1)}, u32[]{:S(2)}, u32[]{:S(2)}) async-start(bf16[8,4,16,128]{3,2,1,0:T(8,128)(2,1)} %shard_map.37), calls=%async_computation | async-start | bytes 262144 | tf_op jit(solution)/shard_map/all_to_all | solution.py:268
  13.3 9.7 %shard_map.38 = bf16[32,256,128]{2,1,0:T(8,128)(2,1)} custom-call(bf16[1024,2048]{1,0:T(8,128)(2,1)} %constant.63.clone.table_hbm, bf16[128,16384]{1,0:T(8,128)(2,1)} %resp_hbm), custom_call_target="tpu_custom_call" | custom-call | flops 4294967296 | bytes 12000000 | tf_op jit(solution)/shard_map/pallas_call | solution.py:86
  23.0 0.0 all-to-all-done
  23.0 10.2 %all-to-all-start.1 = ((bf16[32,256,128]{2,1,0:T(8,128)(2,1)}), bf16[32,256,128]{2,1,0:T(8,128)(2,1)S(1)}, u32[]{:S(2)}, u32[]{:S(2)}) async-start(bf16[32,256,128]{2,1,0:T(8,128)(2,1)} %shard_map.38), calls=%async_computation.1 | async-start | bytes 4194304 | tf_op jit(solution)/shard_map/all_to_all | solution.py:271
  33.4 3.1 %collective-permute-start.2 = (bf16[8,16,128]{2,1,0:T(8,128)(2,1)S(1)}, bf16[8,16,128]{2,1,0:T(8,128)(2,1)S(1)}, u32[]{:S(2)}, u32[]{:S(2)}) collective-permute-start(bf16[8,16,128]{2,1,0:T(8,128)(2,1)S(1)} %get-tuple-element.14), channel_id=1, source_target_pairs={{0,192},{8,200},{16,208},{24,216},{32,224},{40,232},{48,240},{56,2... | collective-permute-start | bytes 98312 | tf_op jit(solution)/shard_map/ppermute | solution.py:155
  36.6 0.8 collective-permute-start.1
  37.4 0.9 collective-permute-start
  38.2 0.8 collective-permute-done.2
  39.0 3.2 %collective-permute-done.1 = bf16[8,16,128]{2,1,0:T(8,128)(2,1)S(1)} collective-permute-done((bf16[8,16,128]{2,1,0:T(8,128)(2,1)S(1)}, bf16[8,16,128]{2,1,0:T(8,128)(2,1)S(1)}, u32[]{:S(2)}, u32[]{:S(2)}) %collective-permute-start.1) | collective-permute-done | bytes 32800 | tf_op jit(solution)/shard_map/ppermute | solution.py:155
  42.2 0.3 collective-permute-done
  42.6 14.4 %all_gather.3.ref_ref = bf16[8,256,128]{2,1,0:T(8,128)(2,1)} all-gather(bf16[1,256,128]{2,1,0:T(8,128)(2,1)S(1)} %bitcast.18), channel_id=1, replica_groups=mesh['seg'=32,'chan'=8] {'chan'}, dimensions={0}, use_global_device_ids=true | all-gather | bytes 589824 | tf_op jit(solution)/shard_map/all_gather | solution.py:157
  57.0 14.4 %shard_map.39.left_ref = bf16[16,192,512]{2,1,0:T(8,128)(2,1)} custom-call(s32[1]{0:T(128)} %bitcast.y_ref, bf16[8,256,128]{2,1,0:T(8,128)(2,1)} %all_gather.3.ref_ref), custom_call_target="tpu_custom_call" | custom-call | flops 6000000000 | bytes 2000000 | tf_op jit(solution)/shard_map/pallas_call | solution.py:232
  71.4 11.6 %all-to-all-done.1.resp_ref = bf16[32,256,128]{2,1,0:T(8,128)(2,1)S(1)} async-done(((bf16[32,256,128]{2,1,0:T(8,128)(2,1)}), bf16[32,256,128]{2,1,0:T(8,128)(2,1)S(1)}, u32[]{:S(2)}, u32[]{:S(2)}) %all-to-all-start.1) | async-done | bytes 2097184 | tf_op jit(solution)/shard_map/all_to_all | solution.py:271
  82.9 0.0 copy-start
  82.9 1.9 %copy-done = bf16[16,192,512]{2,1,0:T(8,128)(2,1)S(1)} copy-done((bf16[16,192,512]{2,1,0:T(8,128)(2,1)S(1)}, bf16[16,192,512]{2,1,0:T(8,128)(2,1)}, u32[]{:S(2)}) %copy-start) | copy-done | bytes 3145752
  84.8 1.8 %shard_map.40 = f32[16,2,32,128]{3,2,1,0:T(8,128)} custom-call(bf16[32,256,128]{2,1,0:T(8,128)(2,1)S(1)} %all-to-all-done.1.resp_ref, bf16[16,192,512]{2,1,0:T(8,128)(2,1)S(1)} %copy-done), custom_call_target="tpu_custom_call" | custom-call | flops 2000000000 | bytes 4000000 | tf_op jit(solution)/shard_map/pallas_call | solution.py:253
  (6 shorter events, 0.1 us)
Async XLA Ops:
  4.8 18.2 %all-to-all-start = ((bf16[8,4,16,128]{3,2,1,0:T(8,128)(2,1)}), bf16[8,4,16,128]{3,2,1,0:T(8,128)(2,1)S(1)}, u32[]{:S(2)}, u32[]{:S(2)}) async-start(bf16[8,4,16,128]{3,2,1,0:T(8,128)(2,1)} %shard_map.37), calls=%async_computation | async-start | bytes 262144 | tf_op jit(solution)/shard_map/all_to_all | solution.py:268
  23.0 59.9 %all-to-all-start.1 = ((bf16[32,256,128]{2,1,0:T(8,128)(2,1)}), bf16[32,256,128]{2,1,0:T(8,128)(2,1)S(1)}, u32[]{:S(2)}, u32[]{:S(2)}) async-start(bf16[32,256,128]{2,1,0:T(8,128)(2,1)} %shard_map.38), calls=%async_computation.1 | async-start | bytes 4194304 | tf_op jit(solution)/shard_map/all_to_all | solution.py:271
  33.4 5.6 %collective-permute-start.2 = (bf16[8,16,128]{2,1,0:T(8,128)(2,1)S(1)}, bf16[8,16,128]{2,1,0:T(8,128)(2,1)S(1)}, u32[]{:S(2)}, u32[]{:S(2)}) collective-permute-start(bf16[8,16,128]{2,1,0:T(8,128)(2,1)S(1)} %get-tuple-element.14), channel_id=1, source_target_pairs={{0,192},{8,200},{16,208},{24,216},{32,224},{40,232},{48,240},{56,2... | collective-permute-start | bytes 98312 | tf_op jit(solution)/shard_map/ppermute | solution.py:155
  36.6 5.6 %collective-permute-start.1 = (bf16[8,16,128]{2,1,0:T(8,128)(2,1)S(1)}, bf16[8,16,128]{2,1,0:T(8,128)(2,1)S(1)}, u32[]{:S(2)}, u32[]{:S(2)}) collective-permute-start(bf16[8,16,128]{2,1,0:T(8,128)(2,1)S(1)} %get-tuple-element.15), channel_id=1, source_target_pairs={{0,128},{8,136},{16,144},{24,152},{32,160},{40,168},{48,176},{56,1... | collective-permute-start | bytes 98312 | tf_op jit(solution)/shard_map/ppermute | solution.py:155
  37.4 5.2 %collective-permute-start = (bf16[8,16,128]{2,1,0:T(8,128)(2,1)S(1)}, bf16[8,16,128]{2,1,0:T(8,128)(2,1)S(1)}, u32[]{:S(2)}, u32[]{:S(2)}) collective-permute-start(bf16[8,16,128]{2,1,0:T(8,128)(2,1)S(1)} %get-tuple-element.16), channel_id=1, source_target_pairs={{0,64},{8,72},{16,80},{24,88},{32,96},{40,104},{48,112},{56,120},{... | collective-permute-start | bytes 98312 | tf_op jit(solution)/shard_map/ppermute | solution.py:155
  82.9 1.9 %copy-start = (bf16[16,192,512]{2,1,0:T(8,128)(2,1)S(1)}, bf16[16,192,512]{2,1,0:T(8,128)(2,1)}, u32[]{:S(2)}) copy-start(bf16[16,192,512]{2,1,0:T(8,128)(2,1)} %shard_map.39.left_ref) | copy-start | bytes 9437188

commit v4 on v3

--- a/solution.py
+++ b/solution.py
@@ -59,13 +59,14 @@
     wanted += [(table_hbm.at[pl.ds(q * rows, rows)], table.at[pl.ds(q * rows, rows)]) for q in range(cuts)]
     wanted += [(resp_hbm.at[:, pl.ds(2 * p * L, 2 * L)], resp.at[p]) for p in range(1, pairs)]
     copies = fetch(wanted, sems)
+    for copy in copies[: 1 + cuts]:
+        copy.wait()
     sent = []
     for p in range(pairs):
-        copies[p + cuts if p else 0].wait()
+        if p:
+            copies[p + cuts].wait()
         pair = jnp.concatenate([resp[p, :, :L], resp[p, :, L:]], axis=0)
         for q in range(cuts):
-            if p == 0:
-                copies[1 + q].wait()
             lines = lax.dot_general(
                 table[q * rows : (q + 1) * rows, :], pair, (((1,), (1,)), ((), ())), preferred_element_type=jnp.float32
             )

time: 87 us -> 86.4 us (level)
  transfers between devices with their start and end apart: 5 -> 5, of which waited for: 4 -> 4; matrix products, arithmetic and copies ran while one was open for 0% -> 0% of each run, Pallas kernels for 28% -> 27%
where the time goes in v4:
time: 86.4 us; the launch traced here: 86 us
  Pallas kernels  30.1 us (35%)
  starting transfers between devices  23.5 us (27%)
  waiting for transfers between devices  15.9 us (18%)
  blocking collectives  14.4 us (17%)
  local copies, waits for them, and re-layouts  1.93 us (2%)
    all_gather x1, blocking collectives, gather_refs(): return lax.all_gather(jnp.stack(got).reshape(NSEG * S, 128), 'chan')  14.4 us
    pallas_call x1, Pallas kernels, invert(): pl.pallas_call(invert_kernel, out_shape=jax.ShapeDtypeStruct((LN, 6 * R,...  14.4 us
    all_to_all x1, waiting for transfers between devices, local(): lines = lax.all_to_all(sent, 'seg', 0, 0, tiled=True)  11.6 us
    all_to_all x1, starting transfers between devices, local(): lines = lax.all_to_all(sent, 'seg', 0, 0, tiled=True)  10.2 us
    pallas_call x1, Pallas kernels, transform(): pl.pallas_call(transform_kernel, in_specs=[away(), away()], out_specs=awa...  9.15 us
    all_to_all x1, starting transfers between devices, local(): lax.all_to_all(tiles, 'seg', 0, 0, axis_index_groups=along_z, tiled=True)  8.48 us
    pallas_call x1, Pallas kernels, ref_transform(): pl.pallas_call(ref_kernel, in_specs=[away(), whole()], out_specs=whole(),...  4.81 us
    ppermute x3, starting transfers between devices, gather_refs(): lax.ppermute(slab, 'seg', [(i, (i + dy * NZ) % NSEG) for i in range(NSEG)])  4.8 us
  transfers between devices with their start and end apart: 5, of which 4 were waited for; matrix products, arithmetic and copies ran while one was open for 0% of the time, Pallas kernels for 27%

profile of v4, /device:TPU:2, one launch (start us, length us, event | category | flops | bytes accessed | tf_op | source)
XLA Modules:
  0.0 86.0 jit_solution(12413074661469047900)
XLA Ops:
  0.0 4.8 %shard_map.37 = bf16[8,4,16,128]{3,2,1,0:T(8,128)(2,1)} custom-call(bf16[1024,2048]{1,0:T(8,128)(2,1)} %constant.63.clone.table_hbm, bf16[4,16384]{1,0:T(4,128)(2,1)} %ref_ref.1), custom_call_target="tpu_custom_call" | custom-call | flops 134217728 | bytes 5000000 | tf_op jit(solution)/shard_map/pallas_call | solution.py:135
  4.8 8.5 %all-to-all-start = ((bf16[8,4,16,128]{3,2,1,0:T(8,128)(2,1)}), bf16[8,4,16,128]{3,2,1,0:T(8,128)(2,1)S(1)}, u32[]{:S(2)}, u32[]{:S(2)}) async-start(bf16[8,4,16,128]{3,2,1,0:T(8,128)(2,1)} %shard_map.37), calls=%async_computation | async-start | bytes 262144 | tf_op jit(solution)/shard_map/all_to_all | solution.py:269
  13.3 9.1 %shard_map.38 = bf16[32,256,128]{2,1,0:T(8,128)(2,1)} custom-call(bf16[1024,2048]{1,0:T(8,128)(2,1)} %constant.63.clone.table_hbm, bf16[128,16384]{1,0:T(8,128)(2,1)} %resp_hbm), custom_call_target="tpu_custom_call" | custom-call | flops 4294967296 | bytes 12000000 | tf_op jit(solution)/shard_map/pallas_call | solution.py:87
  22.4 0.0 all-to-all-done
  22.5 10.2 %all-to-all-start.1 = ((bf16[32,256,128]{2,1,0:T(8,128)(2,1)}), bf16[32,256,128]{2,1,0:T(8,128)(2,1)S(1)}, u32[]{:S(2)}, u32[]{:S(2)}) async-start(bf16[32,256,128]{2,1,0:T(8,128)(2,1)} %shard_map.38), calls=%async_computation.1 | async-start | bytes 4194304 | tf_op jit(solution)/shard_map/all_to_all | solution.py:272
  32.8 3.1 %collective-permute-start.2 = (bf16[8,16,128]{2,1,0:T(8,128)(2,1)S(1)}, bf16[8,16,128]{2,1,0:T(8,128)(2,1)S(1)}, u32[]{:S(2)}, u32[]{:S(2)}) collective-permute-start(bf16[8,16,128]{2,1,0:T(8,128)(2,1)S(1)} %get-tuple-element.14), channel_id=1, source_target_pairs={{0,192},{8,200},{16,208},{24,216},{32,224},{40,232},{48,240},{56,2... | collective-permute-start | bytes 98312 | tf_op jit(solution)/shard_map/ppermute | solution.py:156
  36.0 0.8 collective-permute-start.1
  36.8 0.9 %collective-permute-start = (bf16[8,16,128]{2,1,0:T(8,128)(2,1)S(1)}, bf16[8,16,128]{2,1,0:T(8,128)(2,1)S(1)}, u32[]{:S(2)}, u32[]{:S(2)}) collective-permute-start(bf16[8,16,128]{2,1,0:T(8,128)(2,1)S(1)} %get-tuple-element.16), channel_id=1, source_target_pairs={{0,64},{8,72},{16,80},{24,88},{32,96},{40,104},{48,112},{56,120},{... | collective-permute-start | bytes 98312 | tf_op jit(solution)/shard_map/ppermute | solution.py:156
  37.6 0.8 collective-permute-done.2
  38.4 3.2 %collective-permute-done.1 = bf16[8,16,128]{2,1,0:T(8,128)(2,1)S(1)} collective-permute-done((bf16[8,16,128]{2,1,0:T(8,128)(2,1)S(1)}, bf16[8,16,128]{2,1,0:T(8,128)(2,1)S(1)}, u32[]{:S(2)}, u32[]{:S(2)}) %collective-permute-start.1) | collective-permute-done | bytes 32800 | tf_op jit(solution)/shard_map/ppermute | solution.py:156
  41.6 0.3 collective-permute-done
  42.0 14.4 %all_gather.3.ref_ref = bf16[8,256,128]{2,1,0:T(8,128)(2,1)} all-gather(bf16[1,256,128]{2,1,0:T(8,128)(2,1)S(1)} %bitcast.18), channel_id=1, replica_groups=mesh['seg'=32,'chan'=8] {'chan'}, dimensions={0}, use_global_device_ids=true | all-gather | bytes 589824 | tf_op jit(solution)/shard_map/all_gather | solution.py:158
  56.4 14.4 %shard_map.39.left_ref = bf16[16,192,512]{2,1,0:T(8,128)(2,1)} custom-call(s32[1]{0:T(128)} %bitcast.y_ref, bf16[8,256,128]{2,1,0:T(8,128)(2,1)} %all_gather.3.ref_ref), custom_call_target="tpu_custom_call" | custom-call | flops 6000000000 | bytes 2000000 | tf_op jit(solution)/shard_map/pallas_call | solution.py:233
  70.8 11.6 %all-to-all-done.1.resp_ref = bf16[32,256,128]{2,1,0:T(8,128)(2,1)S(1)} async-done(((bf16[32,256,128]{2,1,0:T(8,128)(2,1)}), bf16[32,256,128]{2,1,0:T(8,128)(2,1)S(1)}, u32[]{:S(2)}, u32[]{:S(2)}) %all-to-all-start.1) | async-done | bytes 2097184 | tf_op jit(solution)/shard_map/all_to_all | solution.py:272
  82.4 0.0 copy-start
  82.4 1.9 %copy-done = bf16[16,192,512]{2,1,0:T(8,128)(2,1)S(1)} copy-done((bf16[16,192,512]{2,1,0:T(8,128)(2,1)S(1)}, bf16[16,192,512]{2,1,0:T(8,128)(2,1)}, u32[]{:S(2)}) %copy-start) | copy-done | bytes 3145752
  84.3 1.8 %shard_map.40 = f32[16,2,32,128]{3,2,1,0:T(8,128)} custom-call(bf16[32,256,128]{2,1,0:T(8,128)(2,1)S(1)} %all-to-all-done.1.resp_ref, bf16[16,192,512]{2,1,0:T(8,128)(2,1)S(1)} %copy-done), custom_call_target="tpu_custom_call" | custom-call | flops 2000000000 | bytes 4000000 | tf_op jit(solution)/shard_map/pallas_call | solution.py:254
  (6 shorter events, 0.1 us)
Async XLA Ops:
  4.8 17.6 %all-to-all-start = ((bf16[8,4,16,128]{3,2,1,0:T(8,128)(2,1)}), bf16[8,4,16,128]{3,2,1,0:T(8,128)(2,1)S(1)}, u32[]{:S(2)}, u32[]{:S(2)}) async-start(bf16[8,4,16,128]{3,2,1,0:T(8,128)(2,1)} %shard_map.37), calls=%async_computation | async-start | bytes 262144 | tf_op jit(solution)/shard_map/all_to_all | solution.py:269
  22.5 59.9 %all-to-all-start.1 = ((bf16[32,256,128]{2,1,0:T(8,128)(2,1)}), bf16[32,256,128]{2,1,0:T(8,128)(2,1)S(1)}, u32[]{:S(2)}, u32[]{:S(2)}) async-start(bf16[32,256,128]{2,1,0:T(8,128)(2,1)} %shard_map.38), calls=%async_computation.1 | async-start | bytes 4194304 | tf_op jit(solution)/shard_map/all_to_all | solution.py:272
  32.8 5.6 %collective-permute-start.2 = (bf16[8,16,128]{2,1,0:T(8,128)(2,1)S(1)}, bf16[8,16,128]{2,1,0:T(8,128)(2,1)S(1)}, u32[]{:S(2)}, u32[]{:S(2)}) collective-permute-start(bf16[8,16,128]{2,1,0:T(8,128)(2,1)S(1)} %get-tuple-element.14), channel_id=1, source_target_pairs={{0,192},{8,200},{16,208},{24,216},{32,224},{40,232},{48,240},{56,2... | collective-permute-start | bytes 98312 | tf_op jit(solution)/shard_map/ppermute | solution.py:156
  36.0 5.6 %collective-permute-start.1 = (bf16[8,16,128]{2,1,0:T(8,128)(2,1)S(1)}, bf16[8,16,128]{2,1,0:T(8,128)(2,1)S(1)}, u32[]{:S(2)}, u32[]{:S(2)}) collective-permute-start(bf16[8,16,128]{2,1,0:T(8,128)(2,1)S(1)} %get-tuple-element.15), channel_id=1, source_target_pairs={{0,128},{8,136},{16,144},{24,152},{32,160},{40,168},{48,176},{56,1... | collective-permute-start | bytes 98312 | tf_op jit(solution)/shard_map/ppermute | solution.py:156
  36.8 5.2 %collective-permute-start = (bf16[8,16,128]{2,1,0:T(8,128)(2,1)S(1)}, bf16[8,16,128]{2,1,0:T(8,128)(2,1)S(1)}, u32[]{:S(2)}, u32[]{:S(2)}) collective-permute-start(bf16[8,16,128]{2,1,0:T(8,128)(2,1)S(1)} %get-tuple-element.16), channel_id=1, source_target_pairs={{0,64},{8,72},{16,80},{24,88},{32,96},{40,104},{48,112},{56,120},{... | collective-permute-start | bytes 98312 | tf_op jit(solution)/shard_map/ppermute | solution.py:156
  82.4 1.9 %copy-start = (bf16[16,192,512]{2,1,0:T(8,128)(2,1)S(1)}, bf16[16,192,512]{2,1,0:T(8,128)(2,1)}, u32[]{:S(2)}) copy-start(bf16[16,192,512]{2,1,0:T(8,128)(2,1)} %shard_map.39.left_ref) | copy-start | bytes 9437188

commit v5 on v4

--- a/solution.py
+++ b/solution.py
@@ -63,8 +63,9 @@
         copy.wait()
     sent = []
     for p in range(pairs):
-        if p:
-            copies[p + cuts].wait()
+        if p == 1:
+            for copy in copies[1 + cuts :]:
+                copy.wait()
         pair = jnp.concatenate([resp[p, :, :L], resp[p, :, L:]], axis=0)
         for q in range(cuts):
             lines = lax.dot_general(

time: 86.4 us -> 86 us (level)
  transfers between devices with their start and end apart: 5 -> 5, of which waited for: 4 -> 5; matrix products, arithmetic and copies ran while one was open for 0% -> 0% of each run, Pallas kernels for 27% -> 27%
where the time goes in v5:
time: 86 us; the launch traced here: 85.6 us
  Pallas kernels  29.7 us (35%)
  starting transfers between devices  23.2 us (27%)
  waiting for transfers between devices  16.2 us (19%)
  blocking collectives  14.4 us (17%)
  local copies, waits for them, and re-layouts  1.93 us (2%)
    all_gather x1, blocking collectives, gather_refs(): return lax.all_gather(jnp.stack(got).reshape(NSEG * S, 128), 'chan')  14.4 us
    pallas_call x1, Pallas kernels, invert(): pl.pallas_call(invert_kernel, out_shape=jax.ShapeDtypeStruct((LN, 6 * R,...  14.4 us
    all_to_all x1, waiting for transfers between devices, local(): lines = lax.all_to_all(sent, 'seg', 0, 0, tiled=True)  11.6 us
    all_to_all x1, starting transfers between devices, local(): lines = lax.all_to_all(sent, 'seg', 0, 0, tiled=True)  9.91 us
    pallas_call x1, Pallas kernels, transform(): pl.pallas_call(transform_kernel, in_specs=[away(), away()], out_specs=awa...  8.76 us
    all_to_all x1, starting transfers between devices, local(): lax.all_to_all(tiles, 'seg', 0, 0, axis_index_groups=along_z, tiled=True)  8.48 us
    pallas_call x1, Pallas kernels, ref_transform(): pl.pallas_call(ref_kernel, in_specs=[away(), whole()], out_specs=whole(),...  4.81 us
    ppermute x3, starting transfers between devices, gather_refs(): lax.ppermute(slab, 'seg', [(i, (i + dy * NZ) % NSEG) for i in range(NSEG)])  4.8 us
  transfers between devices with their start and end apart: 5, of which 5 were waited for; matrix products, arithmetic and copies ran while one was open for 0% of the time, Pallas kernels for 27%

profile of v5, /device:TPU:2, one launch (start us, length us, event | category | flops | bytes accessed | tf_op | source)
XLA Modules:
  0.0 85.6 jit_solution(11953346007217671132)
XLA Ops:
  0.0 4.8 %shard_map.37 = bf16[8,4,16,128]{3,2,1,0:T(8,128)(2,1)} custom-call(bf16[1024,2048]{1,0:T(8,128)(2,1)} %constant.63.clone.table_hbm, bf16[4,16384]{1,0:T(4,128)(2,1)} %ref_ref.1), custom_call_target="tpu_custom_call" | custom-call | flops 134217728 | bytes 5000000 | tf_op jit(solution)/shard_map/pallas_call | solution.py:136
  4.8 8.5 %all-to-all-start = ((bf16[8,4,16,128]{3,2,1,0:T(8,128)(2,1)}), bf16[8,4,16,128]{3,2,1,0:T(8,128)(2,1)S(1)}, u32[]{:S(2)}, u32[]{:S(2)}) async-start(bf16[8,4,16,128]{3,2,1,0:T(8,128)(2,1)} %shard_map.37), calls=%async_computation | async-start | bytes 262144 | tf_op jit(solution)/shard_map/all_to_all | solution.py:270
  13.3 8.8 %shard_map.38 = bf16[32,256,128]{2,1,0:T(8,128)(2,1)} custom-call(bf16[1024,2048]{1,0:T(8,128)(2,1)} %constant.63.clone.table_hbm, bf16[128,16384]{1,0:T(8,128)(2,1)} %resp_hbm), custom_call_target="tpu_custom_call" | custom-call | flops 4294967296 | bytes 12000000 | tf_op jit(solution)/shard_map/pallas_call | solution.py:88
  22.1 0.3 all-to-all-done
  22.4 9.9 %all-to-all-start.1 = ((bf16[32,256,128]{2,1,0:T(8,128)(2,1)}), bf16[32,256,128]{2,1,0:T(8,128)(2,1)S(1)}, u32[]{:S(2)}, u32[]{:S(2)}) async-start(bf16[32,256,128]{2,1,0:T(8,128)(2,1)} %shard_map.38), calls=%async_computation.1 | async-start | bytes 4194304 | tf_op jit(solution)/shard_map/all_to_all | solution.py:273
  32.4 3.1 %collective-permute-start.2 = (bf16[8,16,128]{2,1,0:T(8,128)(2,1)S(1)}, bf16[8,16,128]{2,1,0:T(8,128)(2,1)S(1)}, u32[]{:S(2)}, u32[]{:S(2)}) collective-permute-start(bf16[8,16,128]{2,1,0:T(8,128)(2,1)S(1)} %get-tuple-element.14), channel_id=1, source_target_pairs={{0,192},{8,200},{16,208},{24,216},{32,224},{40,232},{48,240},{56,2... | collective-permute-start | bytes 98312 | tf_op jit(solution)/shard_map/ppermute | solution.py:157
  35.6 0.8 collective-permute-start.1
  36.4 0.9 %collective-permute-start = (bf16[8,16,128]{2,1,0:T(8,128)(2,1)S(1)}, bf16[8,16,128]{2,1,0:T(8,128)(2,1)S(1)}, u32[]{:S(2)}, u32[]{:S(2)}) collective-permute-start(bf16[8,16,128]{2,1,0:T(8,128)(2,1)S(1)} %get-tuple-element.16), channel_id=1, source_target_pairs={{0,64},{8,72},{16,80},{24,88},{32,96},{40,104},{48,112},{56,120},{... | collective-permute-start | bytes 98312 | tf_op jit(solution)/shard_map/ppermute | solution.py:157
  37.2 0.8 collective-permute-done.2
  38.0 3.2 %collective-permute-done.1 = bf16[8,16,128]{2,1,0:T(8,128)(2,1)S(1)} collective-permute-done((bf16[8,16,128]{2,1,0:T(8,128)(2,1)S(1)}, bf16[8,16,128]{2,1,0:T(8,128)(2,1)S(1)}, u32[]{:S(2)}, u32[]{:S(2)}) %collective-permute-start.1) | collective-permute-done | bytes 32800 | tf_op jit(solution)/shard_map/ppermute | solution.py:157
  41.2 0.3 collective-permute-done
  41.6 14.4 %all_gather.3.ref_ref = bf16[8,256,128]{2,1,0:T(8,128)(2,1)} all-gather(bf16[1,256,128]{2,1,0:T(8,128)(2,1)S(1)} %bitcast.18), channel_id=1, replica_groups=mesh['seg'=32,'chan'=8] {'chan'}, dimensions={0}, use_global_device_ids=true | all-gather | bytes 589824 | tf_op jit(solution)/shard_map/all_gather | solution.py:159
  56.0 14.4 %shard_map.39.left_ref = bf16[16,192,512]{2,1,0:T(8,128)(2,1)} custom-call(s32[1]{0:T(128)} %bitcast.y_ref, bf16[8,256,128]{2,1,0:T(8,128)(2,1)} %all_gather.3.ref_ref), custom_call_target="tpu_custom_call" | custom-call | flops 6000000000 | bytes 2000000 | tf_op jit(solution)/shard_map/pallas_call | solution.py:234
  70.4 11.6 %all-to-all-done.1.resp_ref = bf16[32,256,128]{2,1,0:T(8,128)(2,1)S(1)} async-done(((bf16[32,256,128]{2,1,0:T(8,128)(2,1)}), bf16[32,256,128]{2,1,0:T(8,128)(2,1)S(1)}, u32[]{:S(2)}, u32[]{:S(2)}) %all-to-all-start.1) | async-done | bytes 2097184 | tf_op jit(solution)/shard_map/all_to_all | solution.py:273
  82.0 0.0 copy-start
  82.0 1.9 %copy-done = bf16[16,192,512]{2,1,0:T(8,128)(2,1)S(1)} copy-done((bf16[16,192,512]{2,1,0:T(8,128)(2,1)S(1)}, bf16[16,192,512]{2,1,0:T(8,128)(2,1)}, u32[]{:S(2)}) %copy-start) | copy-done | bytes 3145752
  83.9 1.8 %shard_map.40 = f32[16,2,32,128]{3,2,1,0:T(8,128)} custom-call(bf16[32,256,128]{2,1,0:T(8,128)(2,1)S(1)} %all-to-all-done.1.resp_ref, bf16[16,192,512]{2,1,0:T(8,128)(2,1)S(1)} %copy-done), custom_call_target="tpu_custom_call" | custom-call | flops 2000000000 | bytes 4000000 | tf_op jit(solution)/shard_map/pallas_call | solution.py:255
  (6 shorter events, 0.1 us)
Async XLA Ops:
  4.8 17.6 %all-to-all-start = ((bf16[8,4,16,128]{3,2,1,0:T(8,128)(2,1)}), bf16[8,4,16,128]{3,2,1,0:T(8,128)(2,1)S(1)}, u32[]{:S(2)}, u32[]{:S(2)}) async-start(bf16[8,4,16,128]{3,2,1,0:T(8,128)(2,1)} %shard_map.37), calls=%async_computation | async-start | bytes 262144 | tf_op jit(solution)/shard_map/all_to_all | solution.py:270
  22.4 59.6 %all-to-all-start.1 = ((bf16[32,256,128]{2,1,0:T(8,128)(2,1)}), bf16[32,256,128]{2,1,0:T(8,128)(2,1)S(1)}, u32[]{:S(2)}, u32[]{:S(2)}) async-start(bf16[32,256,128]{2,1,0:T(8,128)(2,1)} %shard_map.38), calls=%async_computation.1 | async-start | bytes 4194304 | tf_op jit(solution)/shard_map/all_to_all | solution.py:273
  32.4 5.6 %collective-permute-start.2 = (bf16[8,16,128]{2,1,0:T(8,128)(2,1)S(1)}, bf16[8,16,128]{2,1,0:T(8,128)(2,1)S(1)}, u32[]{:S(2)}, u32[]{:S(2)}) collective-permute-start(bf16[8,16,128]{2,1,0:T(8,128)(2,1)S(1)} %get-tuple-element.14), channel_id=1, source_target_pairs={{0,192},{8,200},{16,208},{24,216},{32,224},{40,232},{48,240},{56,2... | collective-permute-start | bytes 98312 | tf_op jit(solution)/shard_map/ppermute | solution.py:157
  35.6 5.6 %collective-permute-start.1 = (bf16[8,16,128]{2,1,0:T(8,128)(2,1)S(1)}, bf16[8,16,128]{2,1,0:T(8,128)(2,1)S(1)}, u32[]{:S(2)}, u32[]{:S(2)}) collective-permute-start(bf16[8,16,128]{2,1,0:T(8,128)(2,1)S(1)} %get-tuple-element.15), channel_id=1, source_target_pairs={{0,128},{8,136},{16,144},{24,152},{32,160},{40,168},{48,176},{56,1... | collective-permute-start | bytes 98312 | tf_op jit(solution)/shard_map/ppermute | solution.py:157
  36.4 5.2 %collective-permute-start = (bf16[8,16,128]{2,1,0:T(8,128)(2,1)S(1)}, bf16[8,16,128]{2,1,0:T(8,128)(2,1)S(1)}, u32[]{:S(2)}, u32[]{:S(2)}) collective-permute-start(bf16[8,16,128]{2,1,0:T(8,128)(2,1)S(1)} %get-tuple-element.16), channel_id=1, source_target_pairs={{0,64},{8,72},{16,80},{24,88},{32,96},{40,104},{48,112},{56,120},{... | collective-permute-start | bytes 98312 | tf_op jit(solution)/shard_map/ppermute | solution.py:157
  82.0 1.9 %copy-start = (bf16[16,192,512]{2,1,0:T(8,128)(2,1)S(1)}, bf16[16,192,512]{2,1,0:T(8,128)(2,1)}, u32[]{:S(2)}) copy-start(bf16[16,192,512]{2,1,0:T(8,128)(2,1)} %shard_map.39.left_ref) | copy-start | bytes 9437188

commit v6 on v5

--- a/solution.py
+++ b/solution.py
@@ -125,7 +125,6 @@
         )
         for d in range(some):
             tile = jnp.concatenate([spec[r * S : (r + 1) * S, d * w : (d + 1) * w] for r in range(RL)], axis=1)
-            tile = jnp.concatenate([tile, jnp.zeros_like(tile)], axis=0)
             out_ref[d % NZ, q * (some // NZ) + d // NZ] = tile.astype(jnp.bfloat16)
         return carry
 
@@ -137,7 +136,7 @@
         ref_kernel,
         in_specs=[away(), whole()],
         out_specs=whole(),
-        out_shape=jax.ShapeDtypeStruct((NZ, NY, ROWS, 128), jnp.bfloat16),
+        out_shape=jax.ShapeDtypeStruct((NZ, NY, S, 128), jnp.bfloat16),
         scratch_shapes=[
             pltpu.VMEM((2 * FB, L), jnp.bfloat16),
             pltpu.VMEM((RL * S, L), jnp.bfloat16),
@@ -155,7 +154,7 @@
         slab = lax.dynamic_index_in_dim(tiles, (y + dy) % NY, 1, keepdims=False)
         if dy:
             slab = lax.ppermute(slab, "seg", [(i, (i + dy * NZ) % NSEG) for i in range(NSEG)])
-        got.append(slab[:, :S])
+        got.append(slab)
     return lax.all_gather(jnp.stack(got).reshape(NSEG * S, 128), "chan")
 
 

time: 86 us -> 85.9 us (level)
  transfers between devices with their start and end apart: 5 -> 5, of which waited for: 5 -> 4; matrix products, arithmetic and copies ran while one was open for 0% -> 0% of each run, Pallas kernels for 27% -> 27%
where the time goes in v6:
time: 85.9 us; the launch traced here: 85.6 us
  Pallas kernels  29.7 us (35%)
  starting transfers between devices  23.5 us (27%)
  waiting for transfers between devices  15.9 us (19%)
  blocking collectives  14.4 us (17%)
  local copies, waits for them, and re-layouts  1.91 us (2%)
    all_gather x1, blocking collectives, gather_refs(): return lax.all_gather(jnp.stack(got).reshape(NSEG * S, 128), 'chan')  14.4 us
    pallas_call x1, Pallas kernels, invert(): pl.pallas_call(invert_kernel, out_shape=jax.ShapeDtypeStruct((LN, 6 * R,...  14.4 us
    all_to_all x1, waiting for transfers between devices, local(): lines = lax.all_to_all(sent, 'seg', 0, 0, tiled=True)  11.8 us
    all_to_all x1, starting transfers between devices, local(): lines = lax.all_to_all(sent, 'seg', 0, 0, tiled=True)  10.2 us
    pallas_call x1, Pallas kernels, transform(): pl.pallas_call(transform_kernel, in_specs=[away(), away()], out_specs=awa...  8.76 us
    all_to_all x1, starting transfers between devices, local(): lax.all_to_all(tiles, 'seg', 0, 0, axis_index_groups=along_z, tiled=True)  8.48 us
    ppermute x3, starting transfers between devices, gather_refs(): lax.ppermute(slab, 'seg', [(i, (i + dy * NZ) % NSEG) for i in range(NSEG)])  4.8 us
    pallas_call x1, Pallas kernels, ref_transform(): pl.pallas_call(ref_kernel, in_specs=[away(), whole()], out_specs=whole(),...  4.78 us
  transfers between devices with their start and end apart: 5, of which 4 were waited for; matrix products, arithmetic and copies ran while one was open for 0% of the time, Pallas kernels for 27%

profile of v6, /device:TPU:2, one launch (start us, length us, event | category | flops | bytes accessed | tf_op | source)
XLA Modules:
  0.0 85.6 jit_solution(15533496750886079677)
XLA Ops:
  0.0 4.8 %shard_map.37 = bf16[8,4,8,128]{3,2,1,0:T(8,128)(2,1)} custom-call(bf16[1024,2048]{1,0:T(8,128)(2,1)} %constant.63.clone.table_hbm, bf16[4,16384]{1,0:T(4,128)(2,1)} %ref_ref.1), custom_call_target="tpu_custom_call" | custom-call | flops 134217728 | bytes 5000000 | tf_op jit(solution)/shard_map/pallas_call | solution.py:135
  4.8 8.5 %all-to-all-start = ((bf16[8,4,8,128]{3,2,1,0:T(8,128)(2,1)}), bf16[8,4,8,128]{3,2,1,0:T(8,128)(2,1)S(1)}, u32[]{:S(2)}, u32[]{:S(2)}) async-start(bf16[8,4,8,128]{3,2,1,0:T(8,128)(2,1)} %shard_map.37), calls=%async_computation | async-start | bytes 131072 | tf_op jit(solution)/shard_map/all_to_all | solution.py:269
  13.3 8.8 %shard_map.38 = bf16[32,256,128]{2,1,0:T(8,128)(2,1)} custom-call(bf16[1024,2048]{1,0:T(8,128)(2,1)} %constant.63.clone.table_hbm, bf16[128,16384]{1,0:T(8,128)(2,1)} %resp_hbm), custom_call_target="tpu_custom_call" | custom-call | flops 4294967296 | bytes 12000000 | tf_op jit(solution)/shard_map/pallas_call | solution.py:88
  22.0 0.0 all-to-all-done
  22.0 10.2 %all-to-all-start.1 = ((bf16[32,256,128]{2,1,0:T(8,128)(2,1)}), bf16[32,256,128]{2,1,0:T(8,128)(2,1)S(1)}, u32[]{:S(2)}, u32[]{:S(2)}) async-start(bf16[32,256,128]{2,1,0:T(8,128)(2,1)} %shard_map.38), calls=%async_computation.1 | async-start | bytes 4194304 | tf_op jit(solution)/shard_map/all_to_all | solution.py:272
  32.4 3.1 %collective-permute-start.2 = (bf16[8,8,128]{2,1,0:T(8,128)(2,1)S(1)}, bf16[8,8,128]{2,1,0:T(8,128)(2,1)S(1)}, u32[]{:S(2)}, u32[]{:S(2)}) collective-permute-start(bf16[8,8,128]{2,1,0:T(8,128)(2,1)S(1)} %get-tuple-element.14), channel_id=1, source_target_pairs={{0,192},{8,200},{16,208},{24,216},{32,224},{40,232},{48,240},{56,2... | collective-permute-start | bytes 49160 | tf_op jit(solution)/shard_map/ppermute | solution.py:156
  35.5 0.8 collective-permute-start.1
  36.4 0.9 %collective-permute-start = (bf16[8,8,128]{2,1,0:T(8,128)(2,1)S(1)}, bf16[8,8,128]{2,1,0:T(8,128)(2,1)S(1)}, u32[]{:S(2)}, u32[]{:S(2)}) collective-permute-start(bf16[8,8,128]{2,1,0:T(8,128)(2,1)S(1)} %get-tuple-element.16), channel_id=1, source_target_pairs={{0,64},{8,72},{16,80},{24,88},{32,96},{40,104},{48,112},{56,120},{... | collective-permute-start | bytes 49160 | tf_op jit(solution)/shard_map/ppermute | solution.py:156
  37.2 0.3 collective-permute-done.2
  37.5 3.5 %collective-permute-done.1 = bf16[8,8,128]{2,1,0:T(8,128)(2,1)S(1)} collective-permute-done((bf16[8,8,128]{2,1,0:T(8,128)(2,1)S(1)}, bf16[8,8,128]{2,1,0:T(8,128)(2,1)S(1)}, u32[]{:S(2)}, u32[]{:S(2)}) %collective-permute-start.1) | collective-permute-done | bytes 16416 | tf_op jit(solution)/shard_map/ppermute | solution.py:156
  41.0 0.3 collective-permute-done
  41.3 14.4 %all_gather.3.ref_ref = bf16[8,256,128]{2,1,0:T(8,128)(2,1)} all-gather(bf16[1,256,128]{2,1,0:T(8,128)(2,1)S(1)} %bitcast.13), channel_id=1, replica_groups=mesh['seg'=32,'chan'=8] {'chan'}, dimensions={0}, use_global_device_ids=true | all-gather | bytes 589824 | tf_op jit(solution)/shard_map/all_gather | solution.py:158
  55.7 14.4 %shard_map.39.left_ref = bf16[16,192,512]{2,1,0:T(8,128)(2,1)} custom-call(s32[1]{0:T(128)} %bitcast.y_ref, bf16[8,256,128]{2,1,0:T(8,128)(2,1)} %all_gather.3.ref_ref), custom_call_target="tpu_custom_call" | custom-call | flops 6000000000 | bytes 2000000 | tf_op jit(solution)/shard_map/pallas_call | solution.py:233
  70.1 11.8 %all-to-all-done.1.resp_ref = bf16[32,256,128]{2,1,0:T(8,128)(2,1)S(1)} async-done(((bf16[32,256,128]{2,1,0:T(8,128)(2,1)}), bf16[32,256,128]{2,1,0:T(8,128)(2,1)S(1)}, u32[]{:S(2)}, u32[]{:S(2)}) %all-to-all-start.1) | async-done | bytes 2097184 | tf_op jit(solution)/shard_map/all_to_all | solution.py:272
  81.9 0.0 copy-start
  82.0 1.9 %copy-done = bf16[16,192,512]{2,1,0:T(8,128)(2,1)S(1)} copy-done((bf16[16,192,512]{2,1,0:T(8,128)(2,1)S(1)}, bf16[16,192,512]{2,1,0:T(8,128)(2,1)}, u32[]{:S(2)}) %copy-start) | copy-done | bytes 3145752
  83.8 1.8 %shard_map.40 = f32[16,2,32,128]{3,2,1,0:T(8,128)} custom-call(bf16[32,256,128]{2,1,0:T(8,128)(2,1)S(1)} %all-to-all-done.1.resp_ref, bf16[16,192,512]{2,1,0:T(8,128)(2,1)S(1)} %copy-done), custom_call_target="tpu_custom_call" | custom-call | flops 2000000000 | bytes 4000000 | tf_op jit(solution)/shard_map/pallas_call | solution.py:254
  (2 shorter events, 0.0 us)
Async XLA Ops:
  4.8 17.2 %all-to-all-start = ((bf16[8,4,8,128]{3,2,1,0:T(8,128)(2,1)}), bf16[8,4,8,128]{3,2,1,0:T(8,128)(2,1)S(1)}, u32[]{:S(2)}, u32[]{:S(2)}) async-start(bf16[8,4,8,128]{3,2,1,0:T(8,128)(2,1)} %shard_map.37), calls=%async_computation | async-start | bytes 131072 | tf_op jit(solution)/shard_map/all_to_all | solution.py:269
  22.0 59.9 %all-to-all-start.1 = ((bf16[32,256,128]{2,1,0:T(8,128)(2,1)}), bf16[32,256,128]{2,1,0:T(8,128)(2,1)S(1)}, u32[]{:S(2)}, u32[]{:S(2)}) async-start(bf16[32,256,128]{2,1,0:T(8,128)(2,1)} %shard_map.38), calls=%async_computation.1 | async-start | bytes 4194304 | tf_op jit(solution)/shard_map/all_to_all | solution.py:272
  32.4 5.1 %collective-permute-start.2 = (bf16[8,8,128]{2,1,0:T(8,128)(2,1)S(1)}, bf16[8,8,128]{2,1,0:T(8,128)(2,1)S(1)}, u32[]{:S(2)}, u32[]{:S(2)}) collective-permute-start(bf16[8,8,128]{2,1,0:T(8,128)(2,1)S(1)} %get-tuple-element.14), channel_id=1, source_target_pairs={{0,192},{8,200},{16,208},{24,216},{32,224},{40,232},{48,240},{56,2... | collective-permute-start | bytes 49160 | tf_op jit(solution)/shard_map/ppermute | solution.py:156
  35.5 5.4 %collective-permute-start.1 = (bf16[8,8,128]{2,1,0:T(8,128)(2,1)S(1)}, bf16[8,8,128]{2,1,0:T(8,128)(2,1)S(1)}, u32[]{:S(2)}, u32[]{:S(2)}) collective-permute-start(bf16[8,8,128]{2,1,0:T(8,128)(2,1)S(1)} %get-tuple-element.15), channel_id=1, source_target_pairs={{0,128},{8,136},{16,144},{24,152},{32,160},{40,168},{48,176},{56,1... | collective-permute-start | bytes 49160 | tf_op jit(solution)/shard_map/ppermute | solution.py:156
  36.4 4.9 %collective-permute-start = (bf16[8,8,128]{2,1,0:T(8,128)(2,1)S(1)}, bf16[8,8,128]{2,1,0:T(8,128)(2,1)S(1)}, u32[]{:S(2)}, u32[]{:S(2)}) collective-permute-start(bf16[8,8,128]{2,1,0:T(8,128)(2,1)S(1)} %get-tuple-element.16), channel_id=1, source_target_pairs={{0,64},{8,72},{16,80},{24,88},{32,96},{40,104},{48,112},{56,120},{... | collective-permute-start | bytes 49160 | tf_op jit(solution)/shard_map/ppermute | solution.py:156
  81.9 1.9 %copy-start = (bf16[16,192,512]{2,1,0:T(8,128)(2,1)S(1)}, bf16[16,192,512]{2,1,0:T(8,128)(2,1)}, u32[]{:S(2)}) copy-start(bf16[16,192,512]{2,1,0:T(8,128)(2,1)} %shard_map.39.left_ref) | copy-start | bytes 9437188
